TPU v7x, 32 devices: a whole 2x2x4 slice. The times are simulated.
32 devices in a mesh: seq: 16 (over z, y, x), head: 2 (over core).
Axes of the slice: x: 2, y: 2, z: 4, core: 2. Of those that a mesh axis runs over, the one named last changes fastest.
Arguments:
- hidden_in: bfloat16 [2048, 2048], P(('seq', 'head')), may hold values from -6 to 6
- w_inner: bfloat16 [2048, 4096], P(None, 'head'), may hold values from -0.125 to 0.125
- w_inout: bfloat16 [2048, 512], replicated, may hold values from -0.0078125 to 0.0078125
- w_step: bfloat16 [2, 2048, 64], P(None, None, 'head'), may hold values from -0.125 to 0.125
- step_bias: float32 [2, 64], P(None, 'head'), may hold values from -1 to 1
- decay_rate: float32 [64], P('head'), may hold values from 2e-05 to 0.05
- skip_gain: float32 [64], P('head'), may hold values from 0.5 to 1.5
Outputs:
- mixed: bfloat16 [2048, 4096], P('seq', 'head')
All inputs are finite; a program needn't handle non-finite values.
Results may differ from a plain program's by a relative error of at most 0.0052.
Values may be sent and summed in bfloat16 or wider, within the bound.
A program may use at most 128 MiB of HBM per device.

v0:
```python
import jax
import jax.numpy as jnp
from jax import lax
from jax.sharding import PartitionSpec as P

HEADDIM = 64
SPAN = 128


def carried_in(part, axis, combine, identity, reverse):
    count = lax.axis_size(axis)
    place = lax.axis_index(axis)
    ahead = count - 1 - place if reverse else place
    gathered = jax.tree.map(lambda a: lax.all_gather(a, axis), part)
    state = jax.tree.map(lambda a, e: jnp.zeros_like(a) + jnp.asarray(e, a.dtype), part, identity)

    def one(lap, state):
        source = count - 1 - lap if reverse else lap
        return combine(
            state, jax.tree.map(lambda a: lax.dynamic_index_in_dim(a, source, 0, False), gathered)
        )

    return lax.fori_loop(0, ahead, one, state)


def span_pass(inner, in_map, out_map, steps, rate):
    rows, heads_here, width = inner.shape
    count = rows // SPAN
    states = in_map.shape[1]
    exact = lax.Precision.HIGHEST
    values = inner.astype(jnp.float32).reshape(count, SPAN, heads_here, width)
    in_blocks = in_map.astype(jnp.float32).reshape(count, SPAN, states)
    out_blocks = out_map.astype(jnp.float32).reshape(count, SPAN, states)
    logs = (-steps * rate[None, :]).reshape(count, SPAN, heads_here).transpose(0, 2, 1)
    step_blocks = steps.reshape(count, SPAN, heads_here).transpose(0, 2, 1)
    cums = jnp.cumsum(logs, axis=2)
    scores = jnp.einsum("kin,kjn->kij", out_blocks, in_blocks, precision=exact)
    spread = cums[:, :, :, None] - cums[:, :, None, :]
    lower = jnp.arange(SPAN)[:, None] > jnp.arange(SPAN)[None, :]
    decay = jnp.where(lower, jnp.exp(jnp.where(lower, spread, 0.0)), 0.0)
    weights = decay * scores[:, None, :, :] * step_blocks[:, :, None, :]
    intra = jnp.einsum("khij,kjhp->kihp", weights, values, precision=exact)
    tail = jnp.exp(cums[:, :, -1:] - cums) * step_blocks
    pieces = jnp.einsum("khj,kjn,kjhp->khnp", tail, in_blocks, values, precision=exact)
    totals = cums[:, :, -1]

    def advance(carry, item):
        total, piece = item
        return (jnp.exp(total)[:, None, None] * carry + piece, carry)

    last, starts = lax.scan(
        advance, jnp.zeros((heads_here, states, width), jnp.float32), (totals, pieces)
    )
    inter = jnp.einsum("khi,kin,khnp->kihp", jnp.exp(cums), out_blocks, starts, precision=exact)
    before = jnp.cumsum(totals, axis=0) - totals
    reach = cums + before[:, :, None]
    local = (intra + inter).reshape(rows, heads_here, width)
    return (local, last, jnp.exp(jnp.sum(totals, axis=0)), reach)


def incoming(reach, out_map, state, shape):
    count = reach.shape[0]
    out_blocks = out_map.astype(jnp.float32).reshape(count, SPAN, out_map.shape[1])
    added = jnp.einsum(
        "khi,kin,hnp->kihp", jnp.exp(reach), out_blocks, state, precision=lax.Precision.HIGHEST
    )
    return added.reshape(shape)


def combine(earlier, later):
    return (earlier[0] * later[0], later[0][:, None, None] * earlier[1] + later[1])


def shards(hidden_in, w_inner, w_inout, w_step, step_bias, decay_rate, skip_gain):
    heads_here = w_step.shape[2]
    width = w_inner.shape[1]
    states = w_inout.shape[1] // 4
    piece = lax.all_gather(hidden_in, "head", axis=0, tiled=True)
    first = jnp.dot(piece, w_inner, preferred_element_type=jnp.float32)
    second = jnp.dot(piece, w_inout, preferred_element_type=jnp.float32)
    third = jnp.dot(piece, w_step[0], preferred_element_type=jnp.float32)
    fourth = jnp.dot(piece, w_step[1], preferred_element_type=jnp.float32)
    joined = jnp.concatenate([first, second, third, fourth], axis=1)
    rows = joined.shape[0]
    inner = joined[:, :width].astype(jnp.bfloat16).reshape(rows, heads_here, HEADDIM)
    maps = joined[:, width : width + 4 * states].astype(jnp.bfloat16)
    offset = width + 4 * states
    step_fwd = jax.nn.softplus(joined[:, offset : offset + heads_here] + step_bias[0][None, :])
    step_bwd = jax.nn.softplus(
        joined[:, offset + heads_here : offset + 2 * heads_here] + step_bias[1][None, :]
    )
    in_fwd = maps[:, :states]
    out_fwd = maps[:, states : 2 * states]
    in_bwd = jnp.flip(maps[:, 2 * states : 3 * states], 0)
    out_bwd = jnp.flip(maps[:, 3 * states :], 0)
    local_fwd, state_fwd, decay_fwd, reach_fwd = span_pass(
        inner, in_fwd, out_fwd, step_fwd, decay_rate
    )
    local_bwd, state_bwd, decay_bwd, reach_bwd = span_pass(
        jnp.flip(inner, 0), in_bwd, out_bwd, jnp.flip(step_bwd, 0), decay_rate
    )
    identity = (jnp.ones((heads_here,), jnp.float32), jnp.zeros_like(state_fwd))
    before_fwd = carried_in((decay_fwd, state_fwd), "seq", combine, identity, False)
    before_bwd = carried_in((decay_bwd, state_bwd), "seq", combine, identity, True)
    ahead = local_fwd + incoming(reach_fwd, out_fwd, before_fwd[1], local_fwd.shape)
    behind = local_bwd + incoming(reach_bwd, out_bwd, before_bwd[1], local_bwd.shape)
    mixed = ahead + jnp.flip(behind, 0) + skip_gain[None, :, None] * inner.astype(jnp.float32)
    return mixed.reshape(rows, width).astype(jnp.bfloat16)


def solution(mesh):
    placed = (
        P(("seq", "head"), None),
        P(None, "head"),
        P(),
        P(None, None, "head"),
        P(None, "head"),
        P("head"),
        P("head"),
    )
    return jax.shard_map(
        shards, mesh=mesh, in_specs=placed, out_specs=P("seq", "head"), check_vma=False
    )
```

profile of v0, /device:TPU:31, one launch (start us, length us, event | category | flops | bytes accessed | tf_op | source)
XLA Modules:
  0.0 505.9 jit_solution(13691288761053263989)
XLA Ops:
  6.5 2.8 all_gather.19
  13.7 4.6 convolution_convert_fusion
  23.1 30.0 %all-gather.1 = f32[16,32,1]{1,2,0:T(1,128)} all-gather(f32[1,32,1]{1,2,0:T(1,128)S(1)} %get-tuple-element.238), channel_id=3, replica_groups=mesh['seq'=16,'head'=2] {'seq'}, dimensions={0}, use_global_device_ids=true | all-gather | bytes 2176 | tf_op jit(solution)/shard_map/all_gather | solution.py:14
  53.1 32.4 %all-gather = f32[16,32,1]{1,2,0:T(1,128)} all-gather(f32[1,32,1]{1,2,0:T(1,128)S(1)} %get-tuple-element.234), channel_id=2, replica_groups=mesh['seq'=16,'head'=2] {'seq'}, dimensions={0}, use_global_device_ids=true | all-gather | bytes 2176 | tf_op jit(solution)/shard_map/all_gather | solution.py:14
  90.5 120.3 %all-gather.7.cloned.1.call-done = f32[16,32,128,64]{2,3,1,0:T(8,128)} async-done(((f32[1,32,128,64]{2,3,1,0:T(8,128)}), f32[16,32,128,64]{2,3,1,0:T(8,128)}) %all-gather.7.cloned.1.call-update) | async-done | bytes 16777232 | tf_op jit(solution)/shard_map/all_gather | solution.py:14
  215.3 2.4 fusion.39
  219.0 184.4 %all-gather.5.cloned.1.call-done = f32[16,32,128,64]{2,3,1,0:T(8,128)} async-done(((f32[1,32,128,64]{2,3,1,0:T(8,128)}), f32[16,32,128,64]{2,3,1,0:T(8,128)}) %all-gather.5.cloned.1.call-update) | async-done | bytes 16777232 | tf_op jit(solution)/shard_map/all_gather | solution.py:14
  404.9 86.6 %while.16 = (s32[]{:T(128)}, f32[32,128,64]{2,1,0:T(8,128)}, s32[]{:T(128)}, f32[16,32]{1,0:T(8,128)}, f32[16,32,128,64]{2,3,1,0:T(8,128)}, /*index=5*/s32[]{:T(128)}, s32[]{:T(128)}, s32[]{:T(128)}) while((s32[]{:T(128)}, f32[32,128,64]{2,1,0:T(8,128)}, s32[]{:T(128)}, f32[16,32]{1,0:T(8,128)}, f32[16,32,128,64]{2,3,1,0:T(8,128)}, ...), condition=%wide.region_2.3_spmd, body=%wide.region_1.2_spmd.sunk | while | flops 524293 | bytes 7340543 | solution.py:23
  407.5 3.2 bitcast_add_fusion.4
  413.3 3.2 bitcast_add_fusion.4
  419.1 3.2 bitcast_add_fusion.4
  424.8 3.2 bitcast_add_fusion.4
  430.6 3.2 bitcast_add_fusion.4
  436.4 3.2 bitcast_add_fusion.4
  442.1 3.2 bitcast_add_fusion.4
  447.9 3.2 bitcast_add_fusion.4
  453.7 3.2 bitcast_add_fusion.4
  459.4 3.2 bitcast_add_fusion.4
  465.2 3.2 bitcast_add_fusion.4
  471.0 3.2 bitcast_add_fusion.4
  476.8 3.2 bitcast_add_fusion.4
  482.6 3.2 bitcast_add_fusion.4
  488.3 3.2 bitcast_add_fusion.4
  495.3 2.7 fusion.48
  (119 shorter events, 64.7 us)
Async XLA Ops:
  6.5 6.7 %copy-start = (bf16[2048,512]{1,0:T(8,128)(2,1)S(1)}, bf16[2048,512]{1,0:T(8,128)(2,1)}, u32[]{:S(2)}) copy-start(bf16[2048,512]{1,0:T(8,128)(2,1)} %param.13) | copy-start | bytes 6291460
  6.5 6.1 %copy-start.12 = (f32[32]{0:T(128)S(1)}, f32[32]{0:T(128)}, u32[]{:S(2)}) copy-start(f32[32]{0:T(128)} %param.16) | copy-start | bytes 388
  6.5 204.2 %all-gather.7.cloned.1.call-start = ((), (), s32[]{:S(2)}) async-start(), calls=%async_computation.1 | async-start | bytes 17825792 | tf_op jit(solution)/shard_map/all_gather | solution.py:14
  18.7 4.4 copy-start.2
  19.1 4.0 copy-start.4
  20.8 382.6 %all-gather.5.cloned.1.call-start = ((), (), s32[]{:S(2)}) async-start(), calls=%async_computation | async-start | bytes 17825792 | tf_op jit(solution)/shard_map/all_gather | solution.py:14
  212.3 2.9 copy-start.5
  212.3 2.9 copy-start.7
  212.3 2.9 copy-start.9
  212.3 2.9 copy-start.10
  491.5 2.9 copy-start.3
  491.5 2.9 copy-start.11
  491.5 2.9 copy-start.13
  493.8 1.2 copy-start.6
  493.8 1.5 copy-start.8
  495.3 3.7 copy-start.1
Sparse Core Ops, SparseCore 0:
  20.9 189.7 all-gather.6
  213.5 189.7 all-gather.4
where the time goes:
time: 508 us; the launch traced here: 506 us
  waiting for transfers between devices  305 us (60%)
  blocking collectives  65.1 us (13%)
  local copies, waits for them, and re-layouts  51.6 us (10%)
  other arithmetic  49.9 us (10%)
  matrix products  20.6 us (4%)
  between operations  13.7 us (3%)
    all_gather x2, waiting for transfers between devices, carried_in(): gathered = jax.tree.map(lambda a: lax.all_gather(a, axis), part)  305 us
    all_gather x2, blocking collectives, carried_in(): gathered = jax.tree.map(lambda a: lax.all_gather(a, axis), part)  62.3 us
    add x15, other arithmetic, combine(): later[0][:, None, None] * earlier[1] + later[1]  47.7 us
    dynamic_slice x30, local copies, waits for them, and re-layouts, one(): lax.dynamic_index_in_dim(a, source, 0, False)  28.5 us
    mul x15, local copies, waits for them, and re-layouts, combine(): later[0][:, None, None] * earlier[1] + later[1]  10.2 us
  transfers between devices with their start and end apart: 2, of which 2 were waited for; matrix products, arithmetic and copies ran while one was open for 3% of the time, Pallas kernels for 0%

commit v1 on v0

v1 whole, which is shorter than its diff:
```python
import functools

import jax
import jax.numpy as jnp
from jax import lax
from jax.experimental import pallas as pl
from jax.experimental.pallas import tpu as pltpu
from jax.sharding import PartitionSpec as P

HEADDIM = 64
GROUP = 4
MESH = pl.DeviceIdType.MESH
F32 = jnp.float32
BF16 = jnp.bfloat16
EXACT = lax.Precision.HIGHEST


def bdot(a, b):
    return jnp.dot(a, b, preferred_element_type=F32)


def turned(a, b):
    return lax.dot_general(
        a, b, (((0,), (0,)), ((), ())), precision=EXACT, preferred_element_type=F32
    )


def softplus(x):
    return jnp.maximum(x, 0.0) + jnp.log1p(jnp.exp(-jnp.abs(x)))


def kernel(
    ns, nh, rows, dim, width, heads, states, tile, chunk,
    x_ref, w_hbm, wio_hbm, ws_ref, bias_ref, rate_ref, skip_ref, out_ref,
    hid, w_ref, wio_ref, inn, st_f, st_b, tot_f, tot_b, own_out, own_scale, acc,
    snd_f, snd_b, rcv_f, rcv_b,
    w_sem, wio_sem, x_sem, peer_send, peer_recv, sib_send, sib_recv,
    fs_sem, fr_sem, bs_sem, br_sem,
):
    s = lax.axis_index("seq")
    h = lax.axis_index("head")
    span = rows * nh
    place = lax.rem(s, GROUP)
    lap = lax.div(s, GROUP)
    laps = ns // GROUP
    first_seq = s - place
    tiles = width // tile
    chunks = width // chunk

    def partner(d):
        px = lax.rem(lax.rem(place, 2) + d % 2, 2)
        py = lax.rem(lax.div(place, 2) + d // 2, 2)
        return py * 2 + px

    def sibling(e):
        return lax.rem(h + e, nh)

    def piece(g, hh):
        return pl.ds(pl.multiple_of((g * nh + hh) * rows, rows), rows)

    w_copies = [
        pltpu.make_async_copy(
            w_hbm.at[:, pl.ds(t * tile, tile)], w_ref.at[:, pl.ds(t * tile, tile)], w_sem.at[t]
        )
        for t in range(tiles)
    ]
    own_copy = pltpu.make_async_copy(x_ref, hid.at[piece(place, h)], x_sem)
    own_copy.start()
    wio_copy = pltpu.make_async_copy(wio_hbm, wio_ref, wio_sem)
    wio_copy.start()
    for c in w_copies:
        c.start()

    barrier = pltpu.get_barrier_semaphore()
    for d in range(1, GROUP):
        pl.semaphore_signal(barrier, 1, device_id=(first_seq + partner(d), h), device_id_type=MESH)
    for e in range(1, nh):
        pl.semaphore_signal(barrier, 1, device_id=(s, sibling(e)), device_id_type=MESH)

    @pl.when(lap > 0)
    def _():
        pl.semaphore_signal(barrier, 1, device_id=(s - GROUP, h), device_id_type=MESH)

    @pl.when(lap < laps - 1)
    def _():
        pl.semaphore_signal(barrier, 1, device_id=(s + GROUP, h), device_id_type=MESH)

    near = jnp.where(lap > 0, 1, 0) + jnp.where(lap < laps - 1, 1, 0)
    pl.semaphore_wait(barrier, GROUP - 1 + nh - 1 + near)

    peers = [
        pltpu.make_async_remote_copy(
            src_ref=x_ref,
            dst_ref=hid.at[piece(place, h)],
            send_sem=peer_send.at[d - 1],
            recv_sem=peer_recv.at[d - 1],
            device_id=(first_seq + partner(d), h),
            device_id_type=MESH,
        )
        for d in range(1, GROUP)
    ]

    def sib_copies(d):
        src = x_ref if d == 0 else hid.at[piece(partner(d), h)]
        return [
            pltpu.make_async_remote_copy(
                src_ref=src,
                dst_ref=hid.at[piece(partner(d), h)],
                send_sem=sib_send.at[d * (nh - 1) + e - 1],
                recv_sem=sib_recv.at[d * (nh - 1) + e - 1],
                device_id=(s, sibling(e)),
                device_id_type=MESH,
            )
            for e in range(1, nh)
        ]

    sibs = [sib_copies(d) for d in range(GROUP)]
    for c in sibs[0]:
        c.start()
    for c in peers:
        c.start()

    @pl.when(lap == 0)
    def _():
        rcv_f[...] = jnp.zeros_like(rcv_f)

    @pl.when(lap == laps - 1)
    def _():
        rcv_b[...] = jnp.zeros_like(rcv_b)

    below = lax.broadcasted_iota(jnp.int32, (span, span), 0)
    right = lax.broadcasted_iota(jnp.int32, (span, span), 1)
    left_half = lax.broadcasted_iota(jnp.int32, (1, 128), 1) < HEADDIM
    tri = jnp.where(below >= right, 1.0, 0.0).astype(F32)
    rate = rate_ref[...]

    def pair(v, i):
        return jnp.where(left_half, v[:, 2 * i : 2 * i + 1], v[:, 2 * i + 1 : 2 * i + 2])

    def spread_row(v, k):
        n = chunk // 128
        return jnp.concatenate([pair(v, k * n + i) for i in range(n)], axis=1)

    def block(g, waits):
        xb = hid[pl.ds(pl.multiple_of(g * span, span), span), :]
        if waits:
            wio_copy.wait()
        maps = bdot(xb, wio_ref[...]).astype(BF16)
        step_f = softplus(bdot(xb, ws_ref[0]) + bias_ref[0:1, :])
        step_b = softplus(bdot(xb, ws_ref[1]) + bias_ref[1:2, :])
        log_f = -rate * step_f
        log_b = -rate * step_b
        cum_f = jnp.dot(tri, log_f, precision=EXACT, preferred_element_type=F32)
        cum_b = jnp.dot(tri, log_b, precision=EXACT, preferred_element_type=F32)
        exc_b = cum_b - log_b
        last_f = cum_f[span - 1 : span, :]
        last_b = cum_b[span - 1 : span, :]
        tot_f[g] = jnp.broadcast_to(last_f, (8, heads))
        tot_b[g] = jnp.broadcast_to(last_b, (8, heads))
        tail_f = jnp.exp(last_f - cum_f) * step_f
        tail_b = jnp.exp(exc_b) * step_b
        in_f = maps[:, :states].astype(F32).T.astype(BF16)
        in_b = maps[:, 2 * states : 3 * states].astype(F32).T.astype(BF16)
        per = tile // 128
        for t in range(tiles):
            if waits:
                w_copies[t].wait()
            values = bdot(xb, w_ref[:, t * tile : (t + 1) * tile]).astype(BF16)
            inn[:, t * tile : (t + 1) * tile] = values
            wide = values.astype(F32)
            ahead = jnp.concatenate([pair(tail_f, t * per + i) for i in range(per)], axis=1)
            behind = jnp.concatenate([pair(tail_b, t * per + i) for i in range(per)], axis=1)
            st_f[g, :, t * tile : (t + 1) * tile] = bdot(in_f, (ahead * wide).astype(BF16))
            st_b[g, :, t * tile : (t + 1) * tile] = bdot(in_b, (behind * wide).astype(BF16))
        return maps, step_f, step_b, cum_f, exc_b, last_b

    def forward(d):
        peers[d - 1].wait_recv()
        for c in sibs[d]:
            c.start()

    own_copy.wait()
    for c in sibs[0]:
        c.wait_recv()
    maps, step_f, step_b, cum_f, exc_b, last_b = block(place, True)
    forward(1)

    out_f = maps[:, states : 2 * states]
    out_b = maps[:, 3 * states :]
    own_out[0] = out_f
    own_out[1] = out_b
    own_scale[0] = jnp.exp(cum_f)
    own_scale[1] = jnp.exp(last_b - exc_b)
    lower = below > right
    contract = (((1,), (1,)), ((), ()))
    score = jnp.where(
        lower,
        lax.dot_general(out_f, maps[:, :states], contract, preferred_element_type=F32),
        lax.dot_general(
            out_b, maps[:, 2 * states : 3 * states], contract, preferred_element_type=F32
        ),
    )
    score = jnp.where(below == right, 0.0, score)
    unit = jnp.where(below == right, 1.0, 0.0).astype(F32)
    cum_row = turned(cum_f, unit)
    exc_row = turned(exc_b, unit)
    step_row_f = turned(step_f, unit)
    step_row_b = turned(step_b, unit)
    skip = skip_ref[...]
    for i in range(heads // 2):
        both = inn[:, i * 128 : (i + 1) * 128]
        parts = []
        for k in (2 * i, 2 * i + 1):
            gap = jnp.where(
                lower,
                cum_f[:, k : k + 1] - cum_row[k : k + 1, :],
                exc_row[k : k + 1, :] - exc_b[:, k : k + 1],
            )
            scale = jnp.where(lower, step_row_f[k : k + 1, :], step_row_b[k : k + 1, :])
            parts.append(bdot((jnp.exp(gap) * (score * scale)).astype(BF16), both))
        acc[:, i * 128 : (i + 1) * 128] = (
            jnp.where(left_half, parts[0], parts[1]) + pair(skip, i) * both.astype(F32)
        )

    for d in range(1, GROUP):
        for c in sibs[d]:
            c.wait_recv()
        if d < GROUP - 1:
            forward(d + 1)
        block(partner(d), False)

    tf = [tot_f[b][0:1, :] for b in range(GROUP)]
    tb = [tot_b[b][0:1, :] for b in range(GROUP)]
    none = jnp.zeros_like(tf[0])

    def between(logs, keep):
        return jnp.exp(sum([jnp.where(keep(b), logs[b], none) for b in range(GROUP)], none))

    all_f = [between(tf, lambda c, b=b: jnp.asarray(c > b)) for b in range(GROUP)]
    all_b = [between(tb, lambda c, b=b: jnp.asarray(c < b)) for b in range(GROUP)]
    whole_f = between(tf, lambda c: jnp.asarray(True))
    whole_b = between(tb, lambda c: jnp.asarray(True))
    mine_f = [
        jnp.where(b < place, between(tf, lambda c, b=b: (c > b) & (c < place)), none)
        for b in range(GROUP)
    ]
    mine_b = [
        jnp.where(b > place, between(tb, lambda c, b=b: (c < b) & (c > place)), none)
        for b in range(GROUP)
    ]
    reach_f = between(tf, lambda c: c < place)
    reach_b = between(tb, lambda c: c > place)

    f_copies = [
        pltpu.make_async_remote_copy(
            src_ref=snd_f.at[k], dst_ref=rcv_f.at[k], send_sem=fs_sem.at[k], recv_sem=fr_sem.at[k],
            device_id=(s + GROUP, h), device_id_type=MESH,
        )
        for k in range(chunks)
    ]
    b_copies = [
        pltpu.make_async_remote_copy(
            src_ref=snd_b.at[k], dst_ref=rcv_b.at[k], send_sem=bs_sem.at[k], recv_sem=br_sem.at[k],
            device_id=(s - GROUP, h), device_id_type=MESH,
        )
        for k in range(chunks)
    ]

    def step(k, st, rcv, snd, copies, got, sent, totals, whole, mine, reach):
        cols = slice(k * chunk, (k + 1) * chunk)

        @pl.when(got)
        def _():
            copies[k].wait_recv()

        @pl.when(sent)
        def _():
            total = spread_row(whole, k) * rcv[k].astype(F32)
            for b in range(GROUP):
                total = total + spread_row(totals[b], k) * st[b, :, cols]
            snd[k] = total.astype(BF16)
            copies[k].start()

        carry = spread_row(reach, k) * rcv[k].astype(F32)
        for b in range(GROUP):
            carry = carry + spread_row(mine[b], k) * st[b, :, cols]
        return carry.astype(BF16)

    for k in range(chunks):
        cols = slice(k * chunk, (k + 1) * chunk)
        ahead = step(
            k, st_f, rcv_f, snd_f, f_copies, lap > 0, lap < laps - 1, all_f, whole_f, mine_f, reach_f
        )
        behind = step(
            k, st_b, rcv_b, snd_b, b_copies, lap < laps - 1, lap > 0, all_b, whole_b, mine_b, reach_b
        )
        result = acc[:, cols] + spread_row(own_scale[0], k) * bdot(own_out[0], ahead)
        result = result + spread_row(own_scale[1], k) * bdot(own_out[1], behind)
        out_ref[:, cols] = result.astype(out_ref.dtype)

    for c in peers:
        c.wait_send()
    for group in sibs:
        for c in group:
            c.wait_send()

    @pl.when(lap < laps - 1)
    def _():
        for c in f_copies:
            c.wait_send()

    @pl.when(lap > 0)
    def _():
        for c in b_copies:
            c.wait_send()


def shards(ns, nh, hidden_in, w_inner, w_inout, w_step, step_bias, decay_rate, skip_gain):
    rows, dim = hidden_in.shape
    width = w_inner.shape[1]
    heads = w_step.shape[2]
    states = w_inout.shape[1] // 4
    span = rows * nh
    tile = 256
    chunk = 256
    tiles, chunks = width // tile, width // chunk
    dma = pltpu.SemaphoreType.DMA
    vmem = pl.BlockSpec(memory_space=pltpu.VMEM)
    hbm = pl.BlockSpec(memory_space=pl.ANY)
    return pl.pallas_call(
        functools.partial(kernel, ns, nh, rows, dim, width, heads, states, tile, chunk),
        out_shape=jax.ShapeDtypeStruct((span, width), BF16),
        in_specs=[hbm, hbm, hbm, vmem, vmem, vmem, vmem],
        out_specs=vmem,
        scratch_shapes=[
            pltpu.VMEM((GROUP * span, dim), BF16),
            pltpu.VMEM((dim, width), BF16),
            pltpu.VMEM((dim, 4 * states), BF16),
            pltpu.VMEM((span, width), BF16),
            pltpu.VMEM((GROUP, states, width), F32),
            pltpu.VMEM((GROUP, states, width), F32),
            pltpu.VMEM((GROUP, 8, heads), F32),
            pltpu.VMEM((GROUP, 8, heads), F32),
            pltpu.VMEM((2, span, states), BF16),
            pltpu.VMEM((2, span, heads), F32),
            pltpu.VMEM((span, width), F32),
            pltpu.VMEM((chunks, states, chunk), BF16),
            pltpu.VMEM((chunks, states, chunk), BF16),
            pltpu.VMEM((chunks, states, chunk), BF16),
            pltpu.VMEM((chunks, states, chunk), BF16),
            dma((tiles,)),
            dma,
            dma,
            dma((GROUP - 1,)),
            dma((GROUP - 1,)),
            dma((GROUP * (nh - 1),)),
            dma((GROUP * (nh - 1),)),
            dma((chunks,)),
            dma((chunks,)),
            dma((chunks,)),
            dma((chunks,)),
        ],
        compiler_params=pltpu.CompilerParams(
            collective_id=0, has_side_effects=True, vmem_limit_bytes=56 * 1024 * 1024
        ),
    )(
        hidden_in, w_inner, w_inout, w_step, step_bias,
        decay_rate.reshape(1, heads), skip_gain.reshape(1, heads),
    )


def solution(mesh):
    placed = (
        P(("seq", "head"), None),
        P(None, "head"),
        P(),
        P(None, None, "head"),
        P(None, "head"),
        P("head"),
        P("head"),
    )
    return jax.shard_map(
        functools.partial(shards, mesh.shape["seq"], mesh.shape["head"]),
        mesh=mesh, in_specs=placed, out_specs=P("seq", "head"), check_vma=False,
    )
```

time: 508 us -> 200 us (0.39)
  the two profiles are of different devices: /device:TPU:31 before, /device:TPU:0 now
where the time goes in v1:
time: 200 us; the launch traced here: 199 us
  Pallas kernels  195 us (98%)
  local copies, waits for them, and re-layouts  4.17 us (2%)
    pallas_call x1, Pallas kernels, shards(): pl.pallas_call(functools.partial(kernel, ns, nh, rows, dim, width, heads,...  195 us
    unnamed x2, local copies, waits for them, and re-layouts  4.17 us

profile of v1, /device:TPU:0, one launch (start us, length us, event | category | flops | bytes accessed | tf_op | source)
XLA Modules:
  0.0 199.4 jit_solution(11368781181431067457)
XLA Ops:
  0.0 2.3 %copy.8.ws_ref = bf16[2,2048,32]{2,1,0:T(8,128)(2,1)} copy(bf16[2,2048,32]{1,2,0:T(8,128)(2,1)} %param.10) | data formatting | bytes 524288 | tf_op args[3]
  2.3 195.2 %shard_map.73 = bf16[128,2048]{1,0:T(8,128)(2,1)} custom-call(bf16[64,2048]{1,0:T(8,128)(2,1)} %x_ref.1, bf16[2048,2048]{1,0:T(8,128)(2,1)} %w_hbm.1, bf16[2048,512]{1,0:T(8,128)(2,1)} %wio_hbm.1, bf16[2,2048,32]{2,1,0:T(8,128)(2,1)} %copy.8.ws_ref, f32[2,32]{1,0:T(2,128)} %bias_ref.1, f32[1,32]{1,0:T(1,128)} %bitcast.2, f32[1,32]{1,0:T(1,128)} %bitcast.3), custom_call_target="tpu_custom_call" | custom-call | tf_op jit(solution)/shard_map/pallas_call | solution.py:330
  197.5 1.9 copy.10

commit v2 on v1

v2 whole, which is shorter than its diff:
```python
import functools

import jax
import jax.numpy as jnp
from jax import lax
from jax.experimental import pallas as pl
from jax.experimental.pallas import tpu as pltpu
from jax.sharding import PartitionSpec as P

HEADDIM = 64
GROUP = 4
MESH = pl.DeviceIdType.MESH
F32 = jnp.float32
BF16 = jnp.bfloat16
EXACT = lax.Precision.HIGHEST


def bdot(a, b):
    return jnp.dot(a, b, preferred_element_type=F32)


def turned(a, b):
    return lax.dot_general(
        a, b, (((0,), (0,)), ((), ())), precision=EXACT, preferred_element_type=F32
    )


def softplus(x):
    return jnp.maximum(x, 0.0) + jnp.log1p(jnp.exp(-jnp.abs(x)))


def halves(x):
    top = x.astype(BF16).astype(F32)
    return jnp.concatenate([top, x - top], axis=1).astype(BF16)


def kernel(
    ns, nh, rows, dim, width, heads, states, tile, chunk,
    x_ref, w_hbm, wio_hbm, ws_ref, bias_ref, rate_ref, skip_ref, out_ref,
    hid, w_ref, wio_ref, inn, st_f, st_b, tot_f, tot_b, own_out, own_scale, acc,
    widen, lines, cum_line, exc_line, step_line_f, step_line_b,
    snd_f, snd_b, rcv_f, rcv_b,
    w_sem, wio_sem, x_sem, peer_send, peer_recv, sib_send, sib_recv,
    fs_sem, fr_sem, bs_sem, br_sem,
):
    s = lax.axis_index("seq")
    h = lax.axis_index("head")
    span = rows * nh
    place = lax.rem(s, GROUP)
    lap = lax.div(s, GROUP)
    laps = ns // GROUP
    first_seq = s - place
    tiles = width // tile
    chunks = width // chunk

    def partner(d):
        px = lax.rem(lax.rem(place, 2) + lax.rem(d, 2), 2)
        py = lax.rem(lax.div(place, 2) + lax.div(d, 2), 2)
        return py * 2 + px

    def sibling(e):
        return lax.rem(h + e, nh)

    def piece(g, hh):
        return pl.ds(pl.multiple_of((g * nh + hh) * rows, rows), rows)

    def columns(t, size):
        return pl.ds(pl.multiple_of(t * size, size), size)

    def w_copy(t):
        return pltpu.make_async_copy(
            w_hbm.at[:, columns(t, tile)], w_ref.at[:, columns(t, tile)], w_sem.at[t]
        )

    own_copy = pltpu.make_async_copy(x_ref, hid.at[piece(place, h)], x_sem)
    own_copy.start()
    wio_copy = pltpu.make_async_copy(wio_hbm, wio_ref, wio_sem)
    wio_copy.start()
    for t in range(tiles):
        w_copy(jnp.int32(t)).start()

    barrier = pltpu.get_barrier_semaphore()
    for d in range(1, GROUP):
        to = first_seq + partner(jnp.int32(d))
        pl.semaphore_signal(barrier, 1, device_id=(to, h), device_id_type=MESH)
    for e in range(1, nh):
        pl.semaphore_signal(barrier, 1, device_id=(s, sibling(e)), device_id_type=MESH)

    @pl.when(lap > 0)
    def _():
        pl.semaphore_signal(barrier, 1, device_id=(s - GROUP, h), device_id_type=MESH)

    @pl.when(lap < laps - 1)
    def _():
        pl.semaphore_signal(barrier, 1, device_id=(s + GROUP, h), device_id_type=MESH)

    near = jnp.where(lap > 0, 1, 0) + jnp.where(lap < laps - 1, 1, 0)
    pl.semaphore_wait(barrier, GROUP - 1 + nh - 1 + near)

    def peer(d):
        return pltpu.make_async_remote_copy(
            src_ref=x_ref,
            dst_ref=hid.at[piece(place, h)],
            send_sem=peer_send.at[d - 1],
            recv_sem=peer_recv.at[d - 1],
            device_id=(first_seq + partner(d), h),
            device_id_type=MESH,
        )

    def sib(d, e, src):
        return pltpu.make_async_remote_copy(
            src_ref=src,
            dst_ref=hid.at[piece(partner(d), h)],
            send_sem=sib_send.at[d * (nh - 1) + e - 1],
            recv_sem=sib_recv.at[d * (nh - 1) + e - 1],
            device_id=(s, sibling(e)),
            device_id_type=MESH,
        )

    zero = jnp.int32(0)
    for e in range(1, nh):
        sib(zero, e, x_ref).start()
    for d in range(1, GROUP):
        peer(jnp.int32(d)).start()

    @pl.when(lap == 0)
    def _():
        rcv_f[...] = jnp.zeros_like(rcv_f)

    @pl.when(lap == laps - 1)
    def _():
        rcv_b[...] = jnp.zeros_like(rcv_b)

    below = lax.broadcasted_iota(jnp.int32, (span, span), 0)
    right = lax.broadcasted_iota(jnp.int32, (span, span), 1)
    left_half = lax.broadcasted_iota(jnp.int32, (1, 128), 1) < HEADDIM
    lower = below > right
    level = below == right
    rate = rate_ref[...]

    part = lax.rem(lax.broadcasted_iota(jnp.int32, (2 * heads, width), 0), heads) * HEADDIM
    column = lax.broadcasted_iota(jnp.int32, (2 * heads, width), 1)
    widen[...] = jnp.where((column >= part) & (column < part + HEADDIM), 1.0, 0.0).astype(BF16)

    def forward(d):
        peer(d).wait_recv()
        for e in range(1, nh):
            sib(d, e, hid.at[piece(partner(d), h)]).start()

    def block(d, carry):
        g = partner(d)

        @pl.when(d == 0)
        def _():
            own_copy.wait()
            wio_copy.wait()

        for e in range(1, nh):
            sib(d, e, hid.at[piece(g, h)]).wait_recv()

        @pl.when((d > 0) & (d < GROUP - 1))
        def _():
            forward(d + 1)

        here = pl.ds(pl.multiple_of(g * span, span), span)
        xb = hid[here, :]
        maps = bdot(xb, wio_ref[...]).astype(BF16)
        over = (((1,), (1,)), ((), ()))
        step_f = softplus(
            lax.dot_general(xb, ws_ref[0], over, preferred_element_type=F32) + bias_ref[0:1, :]
        )
        step_b = softplus(
            lax.dot_general(xb, ws_ref[1], over, preferred_element_type=F32) + bias_ref[1:2, :]
        )
        log_f = -rate * step_f
        log_b = -rate * step_b
        tri = jnp.where(below >= right, 1.0, 0.0).astype(F32)
        cum_f = jnp.dot(tri, log_f, precision=EXACT, preferred_element_type=F32)
        cum_b = jnp.dot(tri, log_b, precision=EXACT, preferred_element_type=F32)
        exc_b = cum_b - log_b
        last_f = cum_f[span - 1 : span, :]
        last_b = cum_b[span - 1 : span, :]
        tot_f[g] = jnp.broadcast_to(last_f, (8, heads))
        tot_b[g] = jnp.broadcast_to(last_b, (8, heads))
        tail_f = halves(jnp.exp(last_f - cum_f) * step_f)
        tail_b = halves(jnp.exp(exc_b) * step_b)
        in_f = maps[:, :states].astype(F32).T.astype(BF16)
        in_b = maps[:, 2 * states : 3 * states].astype(F32).T.astype(BF16)

        def project(t, carry):
            cols = columns(t, tile)

            @pl.when(d == 0)
            def _():
                w_copy(t).wait()

            values = bdot(hid[here, :], w_ref[:, cols]).astype(BF16)
            inn[:, cols] = values
            wide = values.astype(F32)
            grow = widen[:, cols]
            st_f[g, :, cols] = bdot(in_f, (bdot(tail_f, grow) * wide).astype(BF16))
            st_b[g, :, cols] = bdot(in_b, (bdot(tail_b, grow) * wide).astype(BF16))
            return carry

        lax.fori_loop(0, tiles, project, 0)

        @pl.when(d == 0)
        def _():
            forward(d + 1)
            out_f = maps[:, states : 2 * states]
            out_b = maps[:, 3 * states :]
            own_out[0] = out_f
            own_out[1] = out_b
            own_scale[0] = halves(jnp.exp(cum_f))
            own_scale[1] = halves(jnp.exp(last_b - exc_b))
            score = jnp.where(
                lower,
                lax.dot_general(out_f, maps[:, :states], over, preferred_element_type=F32),
                lax.dot_general(
                    out_b, maps[:, 2 * states : 3 * states], over, preferred_element_type=F32
                ),
            )
            score = jnp.where(level, 0.0, score)
            unit = jnp.where(level, 1.0, 0.0).astype(F32)
            cum_line[...] = turned(cum_f, unit)
            exc_line[...] = turned(exc_b, unit)
            step_line_f[...] = turned(step_f, unit)
            step_line_b[...] = turned(step_b, unit)
            cum_two = halves(cum_f)
            exc_two = halves(exc_b)
            skip_two = halves(jnp.broadcast_to(skip_ref[...], (8, heads)))
            owner = lax.rem(lax.broadcasted_iota(jnp.int32, (2 * heads, 128), 0), heads)

            def mix(i, carry):
                cols = columns(i, 128)
                both = inn[:, cols]
                parts = []
                for k in (2 * i, 2 * i + 1):
                    pick = jnp.where(owner == k, 1.0, 0.0).astype(BF16)
                    one = pl.ds(k, 1)
                    gap = jnp.where(
                        lower,
                        bdot(cum_two, pick) - cum_line[one, :],
                        exc_line[one, :] - bdot(exc_two, pick),
                    )
                    scale = jnp.where(lower, step_line_f[one, :], step_line_b[one, :])
                    parts.append(bdot((jnp.exp(gap) * (score * scale)).astype(BF16), both))
                gain = bdot(skip_two, widen[:, cols])[0:1, :]
                acc[:, cols] = jnp.where(left_half, parts[0], parts[1]) + gain * both.astype(F32)
                return carry

            lax.fori_loop(0, heads // 2, mix, 0)

        return carry

    lax.fori_loop(0, GROUP, block, 0)

    tf = [tot_f[b][0:1, :] for b in range(GROUP)]
    tb = [tot_b[b][0:1, :] for b in range(GROUP)]
    none = jnp.zeros_like(tf[0])

    def between(logs, keep):
        return jnp.exp(sum([jnp.where(keep(b), logs[b], none) for b in range(GROUP)], none))

    all_f = [between(tf, lambda c, b=b: jnp.asarray(c > b)) for b in range(GROUP)]
    all_b = [between(tb, lambda c, b=b: jnp.asarray(c < b)) for b in range(GROUP)]
    whole_f = between(tf, lambda c: jnp.asarray(True))
    whole_b = between(tb, lambda c: jnp.asarray(True))
    mine_f = [
        jnp.where(b < place, between(tf, lambda c, b=b: (c > b) & (c < place)), none)
        for b in range(GROUP)
    ]
    mine_b = [
        jnp.where(b > place, between(tb, lambda c, b=b: (c < b) & (c > place)), none)
        for b in range(GROUP)
    ]
    reach_f = between(tf, lambda c: c < place)
    reach_b = between(tb, lambda c: c > place)
    every = all_f + [whole_f] + mine_f + [reach_f] + all_b + [whole_b] + mine_b + [reach_b]
    every = every + [none] * (-len(every) % 8)
    lines[...] = bdot(halves(jnp.concatenate(every, axis=0)), widen[...])

    def f_copy(k):
        return pltpu.make_async_remote_copy(
            src_ref=snd_f.at[k], dst_ref=rcv_f.at[k], send_sem=fs_sem.at[k], recv_sem=fr_sem.at[k],
            device_id=(s + GROUP, h), device_id_type=MESH,
        )

    def b_copy(k):
        return pltpu.make_async_remote_copy(
            src_ref=snd_b.at[k], dst_ref=rcv_b.at[k], send_sem=bs_sem.at[k], recv_sem=br_sem.at[k],
            device_id=(s - GROUP, h), device_id_type=MESH,
        )

    def step(k, base, st, rcv, snd, copy, got, sent):
        cols = columns(k, chunk)
        line = lines[:, cols]

        def gathered(first):
            total = line[first + GROUP : first + GROUP + 1] * rcv[k].astype(F32)
            for b in range(GROUP):
                total = total + line[first + b : first + b + 1] * st[b, :, cols]
            return total.astype(BF16)

        @pl.when(got)
        def _():
            copy(k).wait_recv()

        @pl.when(sent)
        def _():
            snd[k] = gathered(base)
            copy(k).start()

        return gathered(base + GROUP + 1)

    def finish(k, carry):
        cols = columns(k, chunk)
        ahead = step(k, 0, st_f, rcv_f, snd_f, f_copy, lap > 0, lap < laps - 1)
        behind = step(
            k, 2 * GROUP + 2, st_b, rcv_b, snd_b, b_copy, lap < laps - 1, lap > 0
        )
        grow = widen[:, cols]
        result = acc[:, cols] + bdot(own_scale[0], grow) * bdot(own_out[0], ahead)
        result = result + bdot(own_scale[1], grow) * bdot(own_out[1], behind)
        out_ref[:, cols] = result.astype(out_ref.dtype)
        return carry

    lax.fori_loop(0, chunks, finish, 0)

    for d in range(1, GROUP):
        peer(jnp.int32(d)).wait_send()
    for d in range(GROUP):
        for e in range(1, nh):
            sib(jnp.int32(d), e, x_ref).wait_send()

    @pl.when(lap < laps - 1)
    def _():
        lax.fori_loop(0, chunks, lambda k, c: (f_copy(k).wait_send(), c)[1], 0)

    @pl.when(lap > 0)
    def _():
        lax.fori_loop(0, chunks, lambda k, c: (b_copy(k).wait_send(), c)[1], 0)


def shards(ns, nh, hidden_in, w_inner, w_inout, w_step, step_bias, decay_rate, skip_gain):
    rows, dim = hidden_in.shape
    width = w_inner.shape[1]
    heads = w_step.shape[2]
    states = w_inout.shape[1] // 4
    span = rows * nh
    tile = 512
    chunk = 256
    tiles, chunks = width // tile, width // chunk
    dma = pltpu.SemaphoreType.DMA
    vmem = pl.BlockSpec(memory_space=pltpu.VMEM)
    hbm = pl.BlockSpec(memory_space=pl.ANY)
    return pl.pallas_call(
        functools.partial(kernel, ns, nh, rows, dim, width, heads, states, tile, chunk),
        out_shape=jax.ShapeDtypeStruct((span, width), BF16),
        in_specs=[hbm, hbm, hbm, vmem, vmem, vmem, vmem],
        out_specs=vmem,
        scratch_shapes=[
            pltpu.VMEM((GROUP * span, dim), BF16),
            pltpu.VMEM((dim, width), BF16),
            pltpu.VMEM((dim, 4 * states), BF16),
            pltpu.VMEM((span, width), BF16),
            pltpu.VMEM((GROUP, states, width), F32),
            pltpu.VMEM((GROUP, states, width), F32),
            pltpu.VMEM((GROUP, 8, heads), F32),
            pltpu.VMEM((GROUP, 8, heads), F32),
            pltpu.VMEM((2, span, states), BF16),
            pltpu.VMEM((2, span, 2 * heads), BF16),
            pltpu.VMEM((span, width), F32),
            pltpu.VMEM((2 * heads, width), BF16),
            pltpu.VMEM((24, width), F32),
            pltpu.VMEM((heads, span), F32),
            pltpu.VMEM((heads, span), F32),
            pltpu.VMEM((heads, span), F32),
            pltpu.VMEM((heads, span), F32),
            pltpu.VMEM((chunks, states, chunk), BF16),
            pltpu.VMEM((chunks, states, chunk), BF16),
            pltpu.VMEM((chunks, states, chunk), BF16),
            pltpu.VMEM((chunks, states, chunk), BF16),
            dma((tiles,)),
            dma,
            dma,
            dma((GROUP - 1,)),
            dma((GROUP - 1,)),
            dma((GROUP * (nh - 1),)),
            dma((GROUP * (nh - 1),)),
            dma((chunks,)),
            dma((chunks,)),
            dma((chunks,)),
            dma((chunks,)),
        ],
        compiler_params=pltpu.CompilerParams(
            collective_id=0, has_side_effects=True, vmem_limit_bytes=56 * 1024 * 1024
        ),
    )(
        hidden_in, w_inner, w_inout, jnp.swapaxes(w_step, 1, 2), step_bias,
        decay_rate.reshape(1, heads), skip_gain.reshape(1, heads),
    )


def solution(mesh):
    placed = (
        P(("seq", "head"), None),
        P(None, "head"),
        P(),
        P(None, None, "head"),
        P(None, "head"),
        P("head"),
        P("head"),
    )
    return jax.shard_map(
        functools.partial(shards, mesh.shape["seq"], mesh.shape["head"]),
        mesh=mesh, in_specs=placed, out_specs=P("seq", "head"), check_vma=False,
    )
```

time: 200 us -> 200 us (level)
  Pallas kernels: 195 us -> 198 us
  local copies, waits for them, and re-layouts: 4.17 us -> 1.88 us
    pallas_call x1, Pallas kernels: 195 us -> 198 us  [shards(): pl.pallas_call(functools.partial(kernel, ns, nh, rows, dim, width, heads,...]
    unnamed x2 -> x1, local copies, waits for them, and re-layouts: 4.17 us -> 1.88 us
where the time goes in v2:
time: 200 us
  Pallas kernels  198 us (99%)
    pallas_call x1, Pallas kernels, shards(): pl.pallas_call(functools.partial(kernel, ns, nh, rows, dim, width, heads,...  198 us

profile of v2, /device:TPU:0, one launch (start us, length us, event | category | flops | bytes accessed | tf_op | source)
XLA Modules:
  0.0 199.8 jit_solution(8007856227154021254)
XLA Ops:
  0.0 198.0 %shard_map.73 = bf16[128,2048]{1,0:T(8,128)(2,1)} custom-call(bf16[64,2048]{1,0:T(8,128)(2,1)} %x_ref.1, bf16[2048,2048]{1,0:T(8,128)(2,1)} %w_hbm.1, bf16[2048,512]{1,0:T(8,128)(2,1)} %wio_hbm.1, bf16[2,32,2048]{2,1,0:T(8,128)(2,1)} %bitcast.3, f32[2,32]{1,0:T(2,128)} %bias_ref.1, f32[1,32]{1,0:T(1,128)} %bitcast.4, f32[1,32]{1,0:T(1,128)} %bitcast.5), custom_call_target="tpu_custom_call" | custom-call | tf_op jit(solution)/shard_map/pallas_call | solution.py:357
  198.0 1.9 copy.9

commit v3 on v2

--- a/solution.py
+++ b/solution.py
@@ -292,40 +292,50 @@
             device_id=(s - GROUP, h), device_id_type=MESH,
         )
 
-    def step(k, base, st, rcv, snd, copy, got, sent):
+    def gathered(k, first, st, rcv):
         cols = columns(k, chunk)
         line = lines[:, cols]
-
-        def gathered(first):
-            total = line[first + GROUP : first + GROUP + 1] * rcv[k].astype(F32)
-            for b in range(GROUP):
-                total = total + line[first + b : first + b + 1] * st[b, :, cols]
-            return total.astype(BF16)
-
-        @pl.when(got)
+        total = line[first + GROUP : first + GROUP + 1] * rcv[k].astype(F32)
+        for b in range(GROUP):
+            total = total + line[first + b : first + b + 1] * st[b, :, cols]
+        return total.astype(BF16)
+
+    def pass_on(k, base, st, rcv, snd, copy, got, sent):
+        inside = (k >= 0) & (k < chunks)
+
+        @pl.when(inside & got)
         def _():
             copy(k).wait_recv()
 
-        @pl.when(sent)
-        def _():
-            snd[k] = gathered(base)
+        @pl.when(inside & sent)
+        def _():
+            snd[k] = gathered(k, base, st, rcv)
             copy(k).start()
 
-        return gathered(base + GROUP + 1)
-
-    def finish(k, carry):
-        cols = columns(k, chunk)
-        ahead = step(k, 0, st_f, rcv_f, snd_f, f_copy, lap > 0, lap < laps - 1)
-        behind = step(
-            k, 2 * GROUP + 2, st_b, rcv_b, snd_b, b_copy, lap < laps - 1, lap > 0
-        )
-        grow = widen[:, cols]
-        result = acc[:, cols] + bdot(own_scale[0], grow) * bdot(own_out[0], ahead)
-        result = result + bdot(own_scale[1], grow) * bdot(own_out[1], behind)
-        out_ref[:, cols] = result.astype(out_ref.dtype)
+    lag_f = lap
+    lag_b = laps - 1 - lap
+    lag = jnp.maximum(lag_f, lag_b)
+
+    def slot(n, carry):
+        pass_on(n - lag_f, 0, st_f, rcv_f, snd_f, f_copy, lap > 0, lap < laps - 1)
+        pass_on(
+            n - lag_b, 2 * GROUP + 2, st_b, rcv_b, snd_b, b_copy, lap < laps - 1, lap > 0
+        )
+        k = n - lag
+
+        @pl.when((k >= 0) & (k < chunks))
+        def _():
+            cols = columns(k, chunk)
+            ahead = gathered(k, GROUP + 1, st_f, rcv_f)
+            behind = gathered(k, 3 * GROUP + 3, st_b, rcv_b)
+            grow = widen[:, cols]
+            result = acc[:, cols] + bdot(own_scale[0], grow) * bdot(own_out[0], ahead)
+            result = result + bdot(own_scale[1], grow) * bdot(own_out[1], behind)
+            out_ref[:, cols] = result.astype(out_ref.dtype)
+
         return carry
 
-    lax.fori_loop(0, chunks, finish, 0)
+    lax.fori_loop(0, chunks + laps - 1, slot, 0)
 
     for d in range(1, GROUP):
         peer(jnp.int32(d)).wait_send()

time: 200 us -> 69.5 us (0.35)
  Pallas kernels: 198 us -> 67.4 us
    pallas_call x1, Pallas kernels: 198 us -> 67.4 us  [shards(): pl.pallas_call(functools.partial(kernel, ns, nh, rows, dim, width, heads,...]
where the time goes in v3:
time: 69.5 us; the launch traced here: 69.3 us
  Pallas kernels  67.4 us (97%)
  local copies, waits for them, and re-layouts  1.88 us (3%)
    pallas_call x1, Pallas kernels, shards(): pl.pallas_call(functools.partial(kernel, ns, nh, rows, dim, width, heads,...  67.4 us
    unnamed x1, local copies, waits for them, and re-layouts  1.88 us

profile of v3, /device:TPU:0, one launch (start us, length us, event | category | flops | bytes accessed | tf_op | source)
XLA Modules:
  0.0 69.3 jit_solution(7134206214515760783)
XLA Ops:
  0.0 67.4 %shard_map.73 = bf16[128,2048]{1,0:T(8,128)(2,1)} custom-call(bf16[64,2048]{1,0:T(8,128)(2,1)} %x_ref.1, bf16[2048,2048]{1,0:T(8,128)(2,1)} %w_hbm.1, bf16[2048,512]{1,0:T(8,128)(2,1)} %wio_hbm.1, bf16[2,32,2048]{2,1,0:T(8,128)(2,1)} %bitcast.3, f32[2,32]{1,0:T(2,128)} %bias_ref.1, f32[1,32]{1,0:T(1,128)} %bitcast.4, f32[1,32]{1,0:T(1,128)} %bitcast.5), custom_call_target="tpu_custom_call" | custom-call | tf_op jit(solution)/shard_map/pallas_call | solution.py:367
  67.4 1.9 %copy.9 = bf16[128,2048]{1,0:T(8,128)(2,1)} copy(bf16[128,2048]{1,0:T(8,128)(2,1)} %shard_map.73) | data formatting | bytes 1048576

commit v4 on v3

v4 whole, which is shorter than its diff:
```python
import functools

import jax
import jax.numpy as jnp
from jax import lax
from jax.experimental import pallas as pl
from jax.experimental.pallas import tpu as pltpu
from jax.sharding import PartitionSpec as P

HEADDIM = 64
GROUP = 4
MESH = pl.DeviceIdType.MESH
F32 = jnp.float32
BF16 = jnp.bfloat16
EXACT = lax.Precision.HIGHEST


def bdot(a, b):
    return jnp.dot(a, b, preferred_element_type=F32)


def turned(a, b):
    return lax.dot_general(
        a, b, (((0,), (0,)), ((), ())), precision=EXACT, preferred_element_type=F32
    )


def softplus(x):
    return jnp.maximum(x, 0.0) + jnp.log1p(jnp.exp(-jnp.abs(x)))


def halves(x):
    top = x.astype(BF16).astype(F32)
    return jnp.concatenate([top, x - top], axis=1).astype(BF16)


def kernel(
    ns, nh, rows, dim, width, heads, states, tile, chunk,
    x_ref, w_hbm, wio_hbm, ws_ref, bias_ref, rate_ref, skip_ref, out_ref,
    hid, w_ref, wio_ref, inn, st_f, st_b, own_out, own_scale, acc,
    widen_f, widen_b, lines, cum_line, exc_line, step_line, tails, in_turn,
    snd_f, snd_b, rcv_f, rcv_b,
    w_sem, wio_sem, x_sem, peer_send, peer_recv, sib_send, sib_recv,
    fs_sem, fr_sem, bs_sem, br_sem,
):
    s = lax.axis_index("seq")
    h = lax.axis_index("head")
    span = rows * nh
    place = lax.rem(s, GROUP)
    lap = lax.div(s, GROUP)
    laps = ns // GROUP
    first_seq = s - place
    tiles = width // tile
    chunks = width // chunk

    def partner(d):
        px = lax.rem(lax.rem(place, 2) + lax.rem(d, 2), 2)
        py = lax.rem(lax.div(place, 2) + lax.div(d, 2), 2)
        return py * 2 + px

    def sibling(e):
        return lax.rem(h + e, nh)

    def piece(d, hh):
        return pl.ds(pl.multiple_of((d * nh + hh) * rows, rows), rows)

    def columns(t, size):
        return pl.ds(pl.multiple_of(t * size, size), size)

    def w_copy(t):
        return pltpu.make_async_copy(
            w_hbm.at[:, columns(t, tile)], w_ref.at[:, columns(t, tile)], w_sem.at[t]
        )

    own_copy = pltpu.make_async_copy(x_ref, hid.at[piece(0, h)], x_sem)
    own_copy.start()
    wio_copy = pltpu.make_async_copy(wio_hbm, wio_ref, wio_sem)
    wio_copy.start()
    for t in range(tiles):
        w_copy(jnp.int32(t)).start()

    barrier = pltpu.get_barrier_semaphore()
    for d in range(1, GROUP):
        to = first_seq + partner(jnp.int32(d))
        pl.semaphore_signal(barrier, 1, device_id=(to, h), device_id_type=MESH)
    for e in range(1, nh):
        pl.semaphore_signal(barrier, 1, device_id=(s, sibling(e)), device_id_type=MESH)

    @pl.when(lap > 0)
    def _():
        pl.semaphore_signal(barrier, 1, device_id=(s - GROUP, h), device_id_type=MESH)

    @pl.when(lap < laps - 1)
    def _():
        pl.semaphore_signal(barrier, 1, device_id=(s + GROUP, h), device_id_type=MESH)

    near = jnp.where(lap > 0, 1, 0) + jnp.where(lap < laps - 1, 1, 0)
    pl.semaphore_wait(barrier, GROUP - 1 + nh - 1 + near)

    def peer(d):
        return pltpu.make_async_remote_copy(
            src_ref=x_ref,
            dst_ref=hid.at[piece(d, h)],
            send_sem=peer_send.at[d - 1],
            recv_sem=peer_recv.at[d - 1],
            device_id=(first_seq + partner(d), h),
            device_id_type=MESH,
        )

    def sib(d, e, src):
        return pltpu.make_async_remote_copy(
            src_ref=src,
            dst_ref=hid.at[piece(d, h)],
            send_sem=sib_send.at[d * (nh - 1) + e - 1],
            recv_sem=sib_recv.at[d * (nh - 1) + e - 1],
            device_id=(s, sibling(e)),
            device_id_type=MESH,
        )

    zero = jnp.int32(0)
    for e in range(1, nh):
        sib(zero, e, x_ref).start()
    for d in range(1, GROUP):
        peer(jnp.int32(d)).start()

    @pl.when(lap == 0)
    def _():
        rcv_f[...] = jnp.zeros_like(rcv_f)

    @pl.when(lap == laps - 1)
    def _():
        rcv_b[...] = jnp.zeros_like(rcv_b)

    below = lax.broadcasted_iota(jnp.int32, (span, span), 0)
    right = lax.broadcasted_iota(jnp.int32, (span, span), 1)
    left_half = lax.broadcasted_iota(jnp.int32, (1, 128), 1) < HEADDIM
    lower = below > right
    level = below == right
    tri = jnp.where(below >= right, 1.0, 0.0).astype(F32)
    over = (((1,), (1,)), ((), ()))
    rate = jnp.concatenate([rate_ref[...], rate_ref[...]], axis=1)
    bias = jnp.concatenate([bias_ref[0:1, :], bias_ref[1:2, :]], axis=1)
    two = 2 * heads
    is_fwd = lax.broadcasted_iota(jnp.int32, (span, two), 1) < heads

    part = lax.rem(lax.broadcasted_iota(jnp.int32, (2 * two, width), 0), two) * HEADDIM
    column = lax.broadcasted_iota(jnp.int32, (2 * two, width), 1)
    widen_f[...] = jnp.where((column >= part) & (column < part + HEADDIM), 1.0, 0.0).astype(BF16)
    part = part - width
    widen_b[...] = jnp.where((column >= part) & (column < part + HEADDIM), 1.0, 0.0).astype(BF16)

    def forward(d):
        peer(d).wait_recv()
        for e in range(1, nh):
            sib(d, e, hid.at[piece(d, h)]).start()

    def prepare(xb):
        maps = bdot(xb, wio_ref[...]).astype(BF16)
        steps = softplus(
            lax.dot_general(xb, ws_ref[...], over, preferred_element_type=F32) + bias
        )
        return maps, steps, -rate * steps

    def sums(steps, logs):
        cum = jnp.dot(tri, logs, precision=EXACT, preferred_element_type=F32)
        exc = cum - logs
        last = cum[span - 1 : span, :]
        tail = jnp.exp(jnp.where(is_fwd, last - cum, exc)) * steps
        return cum, exc, last, halves(tail)

    def turn(m):
        return m.astype(F32).T.astype(BF16)

    own_copy.wait()
    for e in range(1, nh):
        sib(zero, e, x_ref).wait_recv()
    wio_copy.wait()
    maps, steps, logs = prepare(hid[0:span, :])
    cum, exc, last_own, tail_own = sums(steps, logs)
    in_f = turn(maps[:, :states])
    in_b = turn(maps[:, 2 * states : 3 * states])

    def project_own(t, carry):
        cols = columns(t, tile)
        w_copy(t).wait()
        values = bdot(hid[0:span, :], w_ref[:, cols]).astype(BF16)
        inn[:, cols] = values
        wide = values.astype(F32)
        st_f[0, :, cols] = bdot(in_f, (bdot(tail_own, widen_f[:, cols]) * wide).astype(BF16))
        st_b[0, :, cols] = bdot(in_b, (bdot(tail_own, widen_b[:, cols]) * wide).astype(BF16))
        return carry

    lax.fori_loop(0, tiles, project_own, 0)
    forward(jnp.int32(1))

    out_f = maps[:, states : 2 * states]
    out_b = maps[:, 3 * states :]
    own_out[0] = out_f
    own_out[1] = out_b
    own_scale[...] = halves(jnp.exp(jnp.where(is_fwd, cum, last_own - exc)))
    score = jnp.where(
        lower,
        lax.dot_general(out_f, maps[:, :states], over, preferred_element_type=F32),
        lax.dot_general(
            out_b, maps[:, 2 * states : 3 * states], over, preferred_element_type=F32
        ),
    )
    score = jnp.where(level, 0.0, score)
    unit = jnp.where(level, 1.0, 0.0).astype(F32)
    cum_line[...] = turned(cum, unit)
    exc_line[...] = turned(exc, unit)
    step_line[...] = turned(steps, unit)
    cum_two = halves(cum)
    exc_two = halves(exc)
    skip_two = halves(
        jnp.broadcast_to(jnp.concatenate([skip_ref[...], skip_ref[...]], axis=1), (8, two))
    )
    owner = lax.rem(lax.broadcasted_iota(jnp.int32, (2 * two, 128), 0), two)

    def mix(i, carry):
        cols = columns(i, 128)
        both = inn[:, cols]
        parts = []
        for k in (2 * i, 2 * i + 1):
            pick_f = jnp.where(owner == k, 1.0, 0.0).astype(BF16)
            pick_b = jnp.where(owner == k + heads, 1.0, 0.0).astype(BF16)
            fwd = pl.ds(k, 1)
            bwd = pl.ds(k + heads, 1)
            gap = jnp.where(
                lower,
                bdot(cum_two, pick_f) - cum_line[fwd, :],
                exc_line[bwd, :] - bdot(exc_two, pick_b),
            )
            scale = jnp.where(lower, step_line[fwd, :], step_line[bwd, :])
            parts.append(bdot((jnp.exp(gap) * (score * scale)).astype(BF16), both))
        gain = bdot(skip_two, widen_f[:, cols])[0:1, :]
        acc[:, cols] = jnp.where(left_half, parts[0], parts[1]) + gain * both.astype(F32)
        return carry

    lax.fori_loop(0, heads // 2, mix, 0)

    for d in range(2, GROUP):
        forward(jnp.int32(d))
    for d in range(1, GROUP):
        for e in range(1, nh):
            sib(jnp.int32(d), e, x_ref).wait_recv()
    maps, steps, logs = prepare(hid[span:, :])
    lasts = [last_own]
    for d in range(1, GROUP):
        mine = slice((d - 1) * span, d * span)
        _, _, last, tail = sums(steps[mine], logs[mine])
        lasts.append(last)
        tails[mine, :] = tail
        in_turn[0, d - 1] = turn(maps[mine, :states])
        in_turn[1, d - 1] = turn(maps[mine, 2 * states : 3 * states])

    def project(k):
        cols = columns(k, chunk)
        wide = bdot(hid[span:, :], w_ref[:, cols]).astype(BF16).astype(F32)
        for way, grow, st in ((0, widen_f, st_f), (1, widen_b, st_b)):
            scaled = (bdot(tails[...], grow[:, cols]) * wide).astype(BF16)
            for d in range(1, GROUP):
                st[d, :, cols] = bdot(in_turn[way, d - 1], scaled[(d - 1) * span : d * span])

    at = [partner(jnp.int32(d)) for d in range(GROUP)]
    none = jnp.zeros_like(last_own)

    def between(keep):
        kept = [jnp.where(keep(at[c]), lasts[c], none) for c in range(GROUP)]
        return jnp.exp(sum(kept, none))

    def always(c):
        return c >= 0

    all_f = [between(lambda c, b=b: c > b) for b in at]
    all_b = [between(lambda c, b=b: c < b) for b in at]
    mine_f = [
        jnp.where(b < place, between(lambda c, b=b: (c > b) & (c < place)), none) for b in at
    ]
    mine_b = [
        jnp.where(b > place, between(lambda c, b=b: (c < b) & (c > place)), none) for b in at
    ]
    every_f = all_f + [between(always)] + mine_f + [between(lambda c: c < place)]
    every_b = all_b + [between(always)] + mine_b + [between(lambda c: c > place)]
    pad = [none] * (16 - len(every_f))
    lines[0:16] = bdot(halves(jnp.concatenate(every_f + pad, axis=0)), widen_f[...])
    lines[16:32] = bdot(halves(jnp.concatenate(every_b + pad, axis=0)), widen_b[...])

    def f_copy(k):
        return pltpu.make_async_remote_copy(
            src_ref=snd_f.at[k], dst_ref=rcv_f.at[k], send_sem=fs_sem.at[k], recv_sem=fr_sem.at[k],
            device_id=(s + GROUP, h), device_id_type=MESH,
        )

    def b_copy(k):
        return pltpu.make_async_remote_copy(
            src_ref=snd_b.at[k], dst_ref=rcv_b.at[k], send_sem=bs_sem.at[k], recv_sem=br_sem.at[k],
            device_id=(s - GROUP, h), device_id_type=MESH,
        )

    def gathered(k, first, st, rcv):
        cols = columns(k, chunk)
        line = lines[:, cols]
        total = line[first + GROUP : first + GROUP + 1] * rcv[k].astype(F32)
        for b in range(GROUP):
            total = total + line[first + b : first + b + 1] * st[b, :, cols]
        return total.astype(BF16)

    def pass_on(k, base, st, rcv, snd, copy, got, sent):
        inside = (k >= 0) & (k < chunks)

        @pl.when(inside & got)
        def _():
            copy(k).wait_recv()

        @pl.when(inside & sent)
        def _():
            snd[k] = gathered(k, base, st, rcv)
            copy(k).start()

    lag_f = lap
    lag_b = laps - 1 - lap
    lag = jnp.maximum(lag_f, lag_b)

    def slot(n, carry):
        @pl.when(n < chunks)
        def _():
            project(n)

        pass_on(n - lag_f, 0, st_f, rcv_f, snd_f, f_copy, lap > 0, lap < laps - 1)
        pass_on(
            n - lag_b, 16, st_b, rcv_b, snd_b, b_copy, lap < laps - 1, lap > 0
        )
        k = n - lag

        @pl.when((k >= 0) & (k < chunks))
        def _():
            cols = columns(k, chunk)
            ahead = gathered(k, GROUP + 1, st_f, rcv_f)
            behind = gathered(k, 16 + GROUP + 1, st_b, rcv_b)
            scale_f = bdot(own_scale[...], widen_f[:, cols])
            scale_b = bdot(own_scale[...], widen_b[:, cols])
            result = acc[:, cols] + scale_f * bdot(own_out[0], ahead)
            result = result + scale_b * bdot(own_out[1], behind)
            out_ref[:, cols] = result.astype(out_ref.dtype)

        return carry

    lax.fori_loop(0, chunks + laps - 1, slot, 0)

    for d in range(1, GROUP):
        peer(jnp.int32(d)).wait_send()
    for d in range(GROUP):
        for e in range(1, nh):
            sib(jnp.int32(d), e, x_ref).wait_send()

    @pl.when(lap < laps - 1)
    def _():
        lax.fori_loop(0, chunks, lambda k, c: (f_copy(k).wait_send(), c)[1], 0)

    @pl.when(lap > 0)
    def _():
        lax.fori_loop(0, chunks, lambda k, c: (b_copy(k).wait_send(), c)[1], 0)


def shards(ns, nh, hidden_in, w_inner, w_inout, w_step, step_bias, decay_rate, skip_gain):
    rows, dim = hidden_in.shape
    width = w_inner.shape[1]
    heads = w_step.shape[2]
    states = w_inout.shape[1] // 4
    span = rows * nh
    tile = 512
    chunk = 256
    tiles, chunks = width // tile, width // chunk
    dma = pltpu.SemaphoreType.DMA
    vmem = pl.BlockSpec(memory_space=pltpu.VMEM)
    hbm = pl.BlockSpec(memory_space=pl.ANY)
    return pl.pallas_call(
        functools.partial(kernel, ns, nh, rows, dim, width, heads, states, tile, chunk),
        out_shape=jax.ShapeDtypeStruct((span, width), BF16),
        in_specs=[hbm, hbm, hbm, vmem, vmem, vmem, vmem],
        out_specs=vmem,
        scratch_shapes=[
            pltpu.VMEM((GROUP * span, dim), BF16),
            pltpu.VMEM((dim, width), BF16),
            pltpu.VMEM((dim, 4 * states), BF16),
            pltpu.VMEM((span, width), BF16),
            pltpu.VMEM((GROUP, states, width), F32),
            pltpu.VMEM((GROUP, states, width), F32),
            pltpu.VMEM((2, span, states), BF16),
            pltpu.VMEM((span, 4 * heads), BF16),
            pltpu.VMEM((span, width), F32),
            pltpu.VMEM((4 * heads, width), BF16),
            pltpu.VMEM((4 * heads, width), BF16),
            pltpu.VMEM((32, width), F32),
            pltpu.VMEM((2 * heads, span), F32),
            pltpu.VMEM((2 * heads, span), F32),
            pltpu.VMEM((2 * heads, span), F32),
            pltpu.VMEM(((GROUP - 1) * span, 4 * heads), BF16),
            pltpu.VMEM((2, GROUP - 1, states, span), BF16),
            pltpu.VMEM((chunks, states, chunk), BF16),
            pltpu.VMEM((chunks, states, chunk), BF16),
            pltpu.VMEM((chunks, states, chunk), BF16),
            pltpu.VMEM((chunks, states, chunk), BF16),
            dma((tiles,)),
            dma,
            dma,
            dma((GROUP - 1,)),
            dma((GROUP - 1,)),
            dma((GROUP * (nh - 1),)),
            dma((GROUP * (nh - 1),)),
            dma((chunks,)),
            dma((chunks,)),
            dma((chunks,)),
            dma((chunks,)),
        ],
        compiler_params=pltpu.CompilerParams(
            collective_id=0, has_side_effects=True, vmem_limit_bytes=56 * 1024 * 1024
        ),
    )(
        hidden_in, w_inner, w_inout,
        jnp.swapaxes(w_step, 1, 2).reshape(2 * heads, dim), step_bias,
        decay_rate.reshape(1, heads), skip_gain.reshape(1, heads),
    )


def solution(mesh):
    placed = (
        P(("seq", "head"), None),
        P(None, "head"),
        P(),
        P(None, None, "head"),
        P(None, "head"),
        P("head"),
        P("head"),
    )
    return jax.shard_map(
        functools.partial(shards, mesh.shape["seq"], mesh.shape["head"]),
        mesh=mesh, in_specs=placed, out_specs=P("seq", "head"), check_vma=False,
    )
```

time: 69.5 us -> 61.6 us (0.89)
  Pallas kernels: 67.4 us -> 59.5 us
    pallas_call x1, Pallas kernels: 67.4 us -> 59.5 us  [shards(): pl.pallas_call(functools.partial(kernel, ns, nh, rows, dim, width, heads,...]
where the time goes in v4:
time: 61.6 us; the launch traced here: 61.4 us
  Pallas kernels  59.5 us (97%)
  local copies, waits for them, and re-layouts  1.88 us (3%)
    pallas_call x1, Pallas kernels, shards(): pl.pallas_call(functools.partial(kernel, ns, nh, rows, dim, width, heads,...  59.5 us
    unnamed x1, local copies, waits for them, and re-layouts  1.88 us

profile of v4, /device:TPU:0, one launch (start us, length us, event | category | flops | bytes accessed | tf_op | source)
XLA Modules:
  0.0 61.4 jit_solution(7853666090563229349)
XLA Ops:
  0.0 59.5 %shard_map.73 = bf16[128,2048]{1,0:T(8,128)(2,1)} custom-call(bf16[64,2048]{1,0:T(8,128)(2,1)} %x_ref.1, bf16[2048,2048]{1,0:T(8,128)(2,1)} %w_hbm.1, bf16[2048,512]{1,0:T(8,128)(2,1)} %wio_hbm.1, bf16[64,2048]{1,0:T(8,128)(2,1)} %bitcast.5, f32[2,32]{1,0:T(2,128)} %bias_ref.1, f32[1,32]{1,0:T(1,128)} %bitcast.6, f32[1,32]{1,0:T(1,128)} %bitcast.7), custom_call_target="tpu_custom_call" | custom-call | tf_op jit(solution)/shard_map/pallas_call | solution.py:378
  59.5 1.9 %copy.9 = bf16[128,2048]{1,0:T(8,128)(2,1)} copy(bf16[128,2048]{1,0:T(8,128)(2,1)} %shard_map.73) | data formatting | bytes 1048576

commit v5 on v4

--- a/solution.py
+++ b/solution.py
@@ -9,6 +9,7 @@
 
 HEADDIM = 64
 GROUP = 4
+STRIDE = 2
 MESH = pl.DeviceIdType.MESH
 F32 = jnp.float32
 BF16 = jnp.bfloat16
@@ -237,10 +238,11 @@
         acc[:, cols] = jnp.where(left_half, parts[0], parts[1]) + gain * both.astype(F32)
         return carry
 
-    lax.fori_loop(0, heads // 2, mix, 0)
-
+    lax.fori_loop(0, heads // 4, mix, 0, unroll=min(4, heads // 4))
     for d in range(2, GROUP):
         forward(jnp.int32(d))
+    lax.fori_loop(heads // 4, heads // 2, mix, 0, unroll=min(4, heads // 4))
+
     for d in range(1, GROUP):
         for e in range(1, nh):
             sib(jnp.int32(d), e, x_ref).wait_recv()
@@ -318,20 +320,20 @@
             snd[k] = gathered(k, base, st, rcv)
             copy(k).start()
 
-    lag_f = lap
-    lag_b = laps - 1 - lap
+    lag_f = STRIDE * lap
+    lag_b = STRIDE * (laps - 1 - lap)
     lag = jnp.maximum(lag_f, lag_b)
 
     def slot(n, carry):
-        @pl.when(n < chunks)
-        def _():
-            project(n)
-
         pass_on(n - lag_f, 0, st_f, rcv_f, snd_f, f_copy, lap > 0, lap < laps - 1)
         pass_on(
             n - lag_b, 16, st_b, rcv_b, snd_b, b_copy, lap < laps - 1, lap > 0
         )
         k = n - lag
+
+        @pl.when(n < chunks - 1)
+        def _():
+            project(n + 1)
 
         @pl.when((k >= 0) & (k < chunks))
         def _():
@@ -346,7 +348,8 @@
 
         return carry
 
-    lax.fori_loop(0, chunks + laps - 1, slot, 0)
+    project(zero)
+    lax.fori_loop(0, chunks + STRIDE * (laps - 1), slot, 0)
 
     for d in range(1, GROUP):
         peer(jnp.int32(d)).wait_send()

time: 61.6 us -> 51.9 us (0.84)
  Pallas kernels: 59.5 us -> 49.9 us
    pallas_call x1, Pallas kernels: 59.5 us -> 49.9 us  [shards(): pl.pallas_call(functools.partial(kernel, ns, nh, rows, dim, width, heads,...]
where the time goes in v5:
time: 51.9 us; the launch traced here: 51.8 us
  Pallas kernels  49.9 us (96%)
  local copies, waits for them, and re-layouts  1.88 us (4%)
    pallas_call x1, Pallas kernels, shards(): pl.pallas_call(functools.partial(kernel, ns, nh, rows, dim, width, heads,...  49.9 us
    unnamed x1, local copies, waits for them, and re-layouts  1.88 us

profile of v5, /device:TPU:0, one launch (start us, length us, event | category | flops | bytes accessed | tf_op | source)
XLA Modules:
  0.0 51.8 jit_solution(8113412927874798412)
XLA Ops:
  0.0 49.9 %shard_map.73 = bf16[128,2048]{1,0:T(8,128)(2,1)} custom-call(bf16[64,2048]{1,0:T(8,128)(2,1)} %x_ref.1, bf16[2048,2048]{1,0:T(8,128)(2,1)} %w_hbm.1, bf16[2048,512]{1,0:T(8,128)(2,1)} %wio_hbm.1, bf16[64,2048]{1,0:T(8,128)(2,1)} %bitcast.5, f32[2,32]{1,0:T(2,128)} %bias_ref.1, f32[1,32]{1,0:T(1,128)} %bitcast.6, f32[1,32]{1,0:T(1,128)} %bitcast.7), custom_call_target="tpu_custom_call" | custom-call | tf_op jit(solution)/shard_map/pallas_call | solution.py:381
  49.9 1.9 %copy.9 = bf16[128,2048]{1,0:T(8,128)(2,1)} copy(bf16[128,2048]{1,0:T(8,128)(2,1)} %shard_map.73) | data formatting | bytes 1048576

commit v6 on v5

--- a/solution.py
+++ b/solution.py
@@ -38,7 +38,7 @@
 def kernel(
     ns, nh, rows, dim, width, heads, states, tile, chunk,
     x_ref, w_hbm, wio_hbm, ws_ref, bias_ref, rate_ref, skip_ref, out_ref,
-    hid, w_ref, wio_ref, inn, st_f, st_b, own_out, own_scale, acc,
+    hid, w_ref, wio_ref, inn, st_f, st_b, own_out, own_scale,
     widen_f, widen_b, lines, cum_line, exc_line, step_line, tails, in_turn,
     snd_f, snd_b, rcv_f, rcv_b,
     w_sem, wio_sem, x_sem, peer_send, peer_recv, sib_send, sib_recv,
@@ -218,7 +218,7 @@
     )
     owner = lax.rem(lax.broadcasted_iota(jnp.int32, (2 * two, 128), 0), two)
 
-    def mix(i, carry):
+    def mix(i):
         cols = columns(i, 128)
         both = inn[:, cols]
         parts = []
@@ -235,26 +235,24 @@
             scale = jnp.where(lower, step_line[fwd, :], step_line[bwd, :])
             parts.append(bdot((jnp.exp(gap) * (score * scale)).astype(BF16), both))
         gain = bdot(skip_two, widen_f[:, cols])[0:1, :]
-        acc[:, cols] = jnp.where(left_half, parts[0], parts[1]) + gain * both.astype(F32)
-        return carry
-
-    lax.fori_loop(0, heads // 4, mix, 0, unroll=min(4, heads // 4))
-    for d in range(2, GROUP):
-        forward(jnp.int32(d))
-    lax.fori_loop(heads // 4, heads // 2, mix, 0, unroll=min(4, heads // 4))
-
-    for d in range(1, GROUP):
+        return jnp.where(left_half, parts[0], parts[1]) + gain * both.astype(F32)
+
+    lasts = [last_own]
+
+    def arrived(d):
         for e in range(1, nh):
             sib(jnp.int32(d), e, x_ref).wait_recv()
-    maps, steps, logs = prepare(hid[span:, :])
-    lasts = [last_own]
+        maps, steps, logs = prepare(hid[d * span : (d + 1) * span, :])
+        _, _, last, tail = sums(steps, logs)
+        lasts.append(last)
+        tails[(d - 1) * span : d * span, :] = tail
+        in_turn[0, d - 1] = turn(maps[:, :states])
+        in_turn[1, d - 1] = turn(maps[:, 2 * states : 3 * states])
+
     for d in range(1, GROUP):
-        mine = slice((d - 1) * span, d * span)
-        _, _, last, tail = sums(steps[mine], logs[mine])
-        lasts.append(last)
-        tails[mine, :] = tail
-        in_turn[0, d - 1] = turn(maps[mine, :states])
-        in_turn[1, d - 1] = turn(maps[mine, 2 * states : 3 * states])
+        if d < GROUP - 1:
+            forward(jnp.int32(d + 1))
+        arrived(d)
 
     def project(k):
         cols = columns(k, chunk)
@@ -342,7 +340,9 @@
             behind = gathered(k, 16 + GROUP + 1, st_b, rcv_b)
             scale_f = bdot(own_scale[...], widen_f[:, cols])
             scale_b = bdot(own_scale[...], widen_b[:, cols])
-            result = acc[:, cols] + scale_f * bdot(own_out[0], ahead)
+            pairs = chunk // 128
+            local = jnp.concatenate([mix(k * pairs + i) for i in range(pairs)], axis=1)
+            result = local + scale_f * bdot(own_out[0], ahead)
             result = result + scale_b * bdot(own_out[1], behind)
             out_ref[:, cols] = result.astype(out_ref.dtype)
 
@@ -392,7 +392,6 @@
             pltpu.VMEM((GROUP, states, width), F32),
             pltpu.VMEM((2, span, states), BF16),
             pltpu.VMEM((span, 4 * heads), BF16),
-            pltpu.VMEM((span, width), F32),
             pltpu.VMEM((4 * heads, width), BF16),
             pltpu.VMEM((4 * heads, width), BF16),
             pltpu.VMEM((32, width), F32),

time: 51.9 us -> 51.4 us (level)
  Pallas kernels: 49.9 us -> 49.3 us
    pallas_call x1, Pallas kernels: 49.9 us -> 49.3 us  [shards(): pl.pallas_call(functools.partial(kernel, ns, nh, rows, dim, width, heads,...]
where the time goes in v6:
time: 51.4 us; the launch traced here: 51.2 us
  Pallas kernels  49.3 us (96%)
  local copies, waits for them, and re-layouts  1.88 us (4%)
    pallas_call x1, Pallas kernels, shards(): pl.pallas_call(functools.partial(kernel, ns, nh, rows, dim, width, heads,...  49.3 us
    unnamed x1, local copies, waits for them, and re-layouts  1.88 us

profile of v6, /device:TPU:0, one launch (start us, length us, event | category | flops | bytes accessed | tf_op | source)
XLA Modules:
  0.0 51.2 jit_solution(17405604172577551264)
XLA Ops:
  0.0 49.3 %shard_map.73 = bf16[128,2048]{1,0:T(8,128)(2,1)} custom-call(bf16[64,2048]{1,0:T(8,128)(2,1)} %x_ref.1, bf16[2048,2048]{1,0:T(8,128)(2,1)} %w_hbm.1, bf16[2048,512]{1,0:T(8,128)(2,1)} %wio_hbm.1, bf16[64,2048]{1,0:T(8,128)(2,1)} %bitcast.5, f32[2,32]{1,0:T(2,128)} %bias_ref.1, f32[1,32]{1,0:T(1,128)} %bitcast.6, f32[1,32]{1,0:T(1,128)} %bitcast.7), custom_call_target="tpu_custom_call" | custom-call | tf_op jit(solution)/shard_map/pallas_call | solution.py:381
  49.3 1.9 %copy.9 = bf16[128,2048]{1,0:T(8,128)(2,1)} copy(bf16[128,2048]{1,0:T(8,128)(2,1)} %shard_map.73) | data formatting | bytes 1048576

commit v7 on v6

--- a/solution.py
+++ b/solution.py
@@ -98,15 +98,25 @@
     near = jnp.where(lap > 0, 1, 0) + jnp.where(lap < laps - 1, 1, 0)
     pl.semaphore_wait(barrier, GROUP - 1 + nh - 1 + near)
 
-    def peer(d):
+    def peer(d, src=x_ref, to=None):
         return pltpu.make_async_remote_copy(
-            src_ref=x_ref,
+            src_ref=src,
             dst_ref=hid.at[piece(d, h)],
             send_sem=peer_send.at[d - 1],
             recv_sem=peer_recv.at[d - 1],
-            device_id=(first_seq + partner(d), h),
+            device_id=(first_seq + partner(d if to is None else to), h),
             device_id_type=MESH,
         )
+
+    def relay():
+        first = 1 + lax.rem(h, 2)
+        peer(first).wait_recv()
+        peer(jnp.int32(3), hid.at[piece(first, h)], 3 - first).start()
+        second = 3 - first
+        peer(second).wait_recv()
+        for d in (first, second):
+            for e in range(1, nh):
+                sib(d, e, hid.at[piece(d, h)]).start()
 
     def sib(d, e, src):
         return pltpu.make_async_remote_copy(
@@ -121,7 +131,7 @@
     zero = jnp.int32(0)
     for e in range(1, nh):
         sib(zero, e, x_ref).start()
-    for d in range(1, GROUP):
+    for d in (1, 2):
         peer(jnp.int32(d)).start()
 
     @pl.when(lap == 0)
@@ -177,6 +187,7 @@
         sib(zero, e, x_ref).wait_recv()
     wio_copy.wait()
     maps, steps, logs = prepare(hid[0:span, :])
+    relay()
     cum, exc, last_own, tail_own = sums(steps, logs)
     in_f = turn(maps[:, :states])
     in_b = turn(maps[:, 2 * states : 3 * states])
@@ -192,7 +203,6 @@
         return carry
 
     lax.fori_loop(0, tiles, project_own, 0)
-    forward(jnp.int32(1))
 
     out_f = maps[:, states : 2 * states]
     out_b = maps[:, 3 * states :]
@@ -250,8 +260,8 @@
         in_turn[1, d - 1] = turn(maps[:, 2 * states : 3 * states])
 
     for d in range(1, GROUP):
-        if d < GROUP - 1:
-            forward(jnp.int32(d + 1))
+        if d == GROUP - 2:
+            forward(jnp.int32(GROUP - 1))
         arrived(d)
 
     def project(k):

time: 51.4 us -> 50.7 us (0.986)
  Pallas kernels: 49.3 us -> 48.6 us
    pallas_call x1, Pallas kernels: 49.3 us -> 48.6 us  [shards(): pl.pallas_call(functools.partial(kernel, ns, nh, rows, dim, width, heads,...]
where the time goes in v7:
time: 50.7 us; the launch traced here: 50.5 us
  Pallas kernels  48.6 us (96%)
  local copies, waits for them, and re-layouts  1.88 us (4%)
    pallas_call x1, Pallas kernels, shards(): pl.pallas_call(functools.partial(kernel, ns, nh, rows, dim, width, heads,...  48.6 us
    unnamed x1, local copies, waits for them, and re-layouts  1.88 us

profile of v7, /device:TPU:0, one launch (start us, length us, event | category | flops | bytes accessed | tf_op | source)
XLA Modules:
  0.0 50.5 jit_solution(9661560357808420381)
XLA Ops:
  0.0 48.6 %shard_map.73 = bf16[128,2048]{1,0:T(8,128)(2,1)} custom-call(bf16[64,2048]{1,0:T(8,128)(2,1)} %x_ref.1, bf16[2048,2048]{1,0:T(8,128)(2,1)} %w_hbm.1, bf16[2048,512]{1,0:T(8,128)(2,1)} %wio_hbm.1, bf16[64,2048]{1,0:T(8,128)(2,1)} %bitcast.5, f32[2,32]{1,0:T(2,128)} %bias_ref.1, f32[1,32]{1,0:T(1,128)} %bitcast.6, f32[1,32]{1,0:T(1,128)} %bitcast.7), custom_call_target="tpu_custom_call" | custom-call | tf_op jit(solution)/shard_map/pallas_call | solution.py:391
  48.6 1.9 %copy.9 = bf16[128,2048]{1,0:T(8,128)(2,1)} copy(bf16[128,2048]{1,0:T(8,128)(2,1)} %shard_map.73) | data formatting | bytes 1048576

commit v8 on v7

--- a/solution.py
+++ b/solution.py
@@ -42,7 +42,7 @@
     widen_f, widen_b, lines, cum_line, exc_line, step_line, tails, in_turn,
     snd_f, snd_b, rcv_f, rcv_b,
     w_sem, wio_sem, x_sem, peer_send, peer_recv, sib_send, sib_recv,
-    fs_sem, fr_sem, bs_sem, br_sem,
+    fs_sem, fr_sem, bs_sem, br_sem, fshare_sem, bshare_sem,
 ):
     s = lax.axis_index("seq")
     h = lax.axis_index("head")
@@ -316,12 +316,40 @@
             total = total + line[first + b : first + b + 1] * st[b, :, cols]
         return total.astype(BF16)
 
-    def pass_on(k, base, st, rcv, snd, copy, got, sent):
-        inside = (k >= 0) & (k < chunks)
+    shared = GROUP if chunks >= 2 * GROUP else 0
+    direct = chunks - shared
+    chained = direct + (1 if shared else 0)
+
+    def chunk_at(p):
+        if not shared:
+            return p
+        other = lax.rem(place + jnp.maximum(p - direct, 0), GROUP)
+        return jnp.where(p == 0, place, jnp.where(p <= direct, shared + p - 1, other))
+
+    def share(rcv, sent, got, d):
+        return pltpu.make_async_remote_copy(
+            src_ref=rcv.at[place],
+            dst_ref=rcv.at[place],
+            send_sem=sent.at[d - 1],
+            recv_sem=got.at[place],
+            device_id=(first_seq + partner(jnp.int32(d)), h),
+            device_id_type=MESH,
+        )
+
+    def pass_on(p, base, st, rcv, snd, copy, got, sent, shared_sem, arrive_sem):
+        inside = (p >= 0) & (p < chained)
+        k = chunk_at(p)
 
         @pl.when(inside & got)
         def _():
             copy(k).wait_recv()
+
+        if shared:
+
+            @pl.when((p == 0) & got)
+            def _():
+                for d in range(1, GROUP):
+                    share(rcv, shared_sem, arrive_sem, d).start()
 
         @pl.when(inside & sent)
         def _():
@@ -331,20 +359,34 @@
     lag_f = STRIDE * lap
     lag_b = STRIDE * (laps - 1 - lap)
     lag = jnp.maximum(lag_f, lag_b)
+    not_first = lap > 0
+    not_last = lap < laps - 1
 
     def slot(n, carry):
-        pass_on(n - lag_f, 0, st_f, rcv_f, snd_f, f_copy, lap > 0, lap < laps - 1)
         pass_on(
-            n - lag_b, 16, st_b, rcv_b, snd_b, b_copy, lap < laps - 1, lap > 0
-        )
-        k = n - lag
+            n - lag_f, 0, st_f, rcv_f, snd_f, f_copy, not_first, not_last, fshare_sem, fr_sem
+        )
+        pass_on(
+            n - lag_b, 16, st_b, rcv_b, snd_b, b_copy, not_last, not_first, bshare_sem, br_sem
+        )
+        p = n - lag
 
         @pl.when(n < chunks - 1)
         def _():
-            project(n + 1)
-
-        @pl.when((k >= 0) & (k < chunks))
+            project(chunk_at(n + 1))
+
+        @pl.when((p >= 0) & (p < chunks))
         def _():
+            k = chunk_at(p)
+
+            @pl.when((p >= chained) & not_first)
+            def _():
+                f_copy(k).wait_recv()
+
+            @pl.when((p >= chained) & not_last)
+            def _():
+                b_copy(k).wait_recv()
+
             cols = columns(k, chunk)
             ahead = gathered(k, GROUP + 1, st_f, rcv_f)
             behind = gathered(k, 16 + GROUP + 1, st_b, rcv_b)
@@ -358,7 +400,7 @@
 
         return carry
 
-    project(zero)
+    project(chunk_at(zero))
     lax.fori_loop(0, chunks + STRIDE * (laps - 1), slot, 0)
 
     for d in range(1, GROUP):
@@ -367,13 +409,20 @@
         for e in range(1, nh):
             sib(jnp.int32(d), e, x_ref).wait_send()
 
-    @pl.when(lap < laps - 1)
-    def _():
-        lax.fori_loop(0, chunks, lambda k, c: (f_copy(k).wait_send(), c)[1], 0)
-
-    @pl.when(lap > 0)
-    def _():
-        lax.fori_loop(0, chunks, lambda k, c: (b_copy(k).wait_send(), c)[1], 0)
+    def sent_all(copy, rcv, shared_sem, arrive_sem, got, sent):
+        @pl.when(sent)
+        def _():
+            lax.fori_loop(0, chained, lambda p, c: (copy(chunk_at(p)).wait_send(), c)[1], 0)
+
+        if shared:
+
+            @pl.when(got)
+            def _():
+                for d in range(1, GROUP):
+                    share(rcv, shared_sem, arrive_sem, d).wait_send()
+
+    sent_all(f_copy, rcv_f, fshare_sem, fr_sem, not_first, not_last)
+    sent_all(b_copy, rcv_b, bshare_sem, br_sem, not_last, not_first)
 
 
 def shards(ns, nh, hidden_in, w_inner, w_inout, w_step, step_bias, decay_rate, skip_gain):
@@ -425,6 +474,8 @@
             dma((chunks,)),
             dma((chunks,)),
             dma((chunks,)),
+            dma((GROUP - 1,)),
+            dma((GROUP - 1,)),
         ],
         compiler_params=pltpu.CompilerParams(
             collective_id=0, has_side_effects=True, vmem_limit_bytes=56 * 1024 * 1024

time: 50.7 us -> 47.1 us (0.929)
  Pallas kernels: 48.6 us -> 45 us
    pallas_call x1, Pallas kernels: 48.6 us -> 45 us  [shards(): pl.pallas_call(functools.partial(kernel, ns, nh, rows, dim, width, heads,...]
where the time goes in v8:
time: 47.1 us; the launch traced here: 46.9 us
  Pallas kernels  45 us (96%)
  local copies, waits for them, and re-layouts  1.88 us (4%)
    pallas_call x1, Pallas kernels, shards(): pl.pallas_call(functools.partial(kernel, ns, nh, rows, dim, width, heads,...  45 us
    unnamed x1, local copies, waits for them, and re-layouts  1.88 us

profile of v8, /device:TPU:0, one launch (start us, length us, event | category | flops | bytes accessed | tf_op | source)
XLA Modules:
  0.0 46.9 jit_solution(6589756192582528227)
XLA Ops:
  0.0 45.0 %shard_map.73 = bf16[128,2048]{1,0:T(8,128)(2,1)} custom-call(bf16[64,2048]{1,0:T(8,128)(2,1)} %x_ref.1, bf16[2048,2048]{1,0:T(8,128)(2,1)} %w_hbm.1, bf16[2048,512]{1,0:T(8,128)(2,1)} %wio_hbm.1, bf16[64,2048]{1,0:T(8,128)(2,1)} %bitcast.5, f32[2,32]{1,0:T(2,128)} %bias_ref.1, f32[1,32]{1,0:T(1,128)} %bitcast.6, f32[1,32]{1,0:T(1,128)} %bitcast.7), custom_call_target="tpu_custom_call" | custom-call | tf_op jit(solution)/shard_map/pallas_call | solution.py:440
  45.0 1.9 %copy.9 = bf16[128,2048]{1,0:T(8,128)(2,1)} copy(bf16[128,2048]{1,0:T(8,128)(2,1)} %shard_map.73) | data formatting | bytes 1048576

commit v9 on v8

--- a/solution.py
+++ b/solution.py
@@ -189,20 +189,9 @@
     maps, steps, logs = prepare(hid[0:span, :])
     relay()
     cum, exc, last_own, tail_own = sums(steps, logs)
-    in_f = turn(maps[:, :states])
-    in_b = turn(maps[:, 2 * states : 3 * states])
-
-    def project_own(t, carry):
-        cols = columns(t, tile)
-        w_copy(t).wait()
-        values = bdot(hid[0:span, :], w_ref[:, cols]).astype(BF16)
-        inn[:, cols] = values
-        wide = values.astype(F32)
-        st_f[0, :, cols] = bdot(in_f, (bdot(tail_own, widen_f[:, cols]) * wide).astype(BF16))
-        st_b[0, :, cols] = bdot(in_b, (bdot(tail_own, widen_b[:, cols]) * wide).astype(BF16))
-        return carry
-
-    lax.fori_loop(0, tiles, project_own, 0)
+    tails[0:span, :] = tail_own
+    in_turn[0, 0] = turn(maps[:, :states])
+    in_turn[1, 0] = turn(maps[:, 2 * states : 3 * states])
 
     out_f = maps[:, states : 2 * states]
     out_b = maps[:, 3 * states :]
@@ -255,9 +244,9 @@
         maps, steps, logs = prepare(hid[d * span : (d + 1) * span, :])
         _, _, last, tail = sums(steps, logs)
         lasts.append(last)
-        tails[(d - 1) * span : d * span, :] = tail
-        in_turn[0, d - 1] = turn(maps[:, :states])
-        in_turn[1, d - 1] = turn(maps[:, 2 * states : 3 * states])
+        tails[d * span : (d + 1) * span, :] = tail
+        in_turn[0, d] = turn(maps[:, :states])
+        in_turn[1, d] = turn(maps[:, 2 * states : 3 * states])
 
     for d in range(1, GROUP):
         if d == GROUP - 2:
@@ -266,11 +255,13 @@
 
     def project(k):
         cols = columns(k, chunk)
-        wide = bdot(hid[span:, :], w_ref[:, cols]).astype(BF16).astype(F32)
+        values = bdot(hid[...], w_ref[:, cols]).astype(BF16)
+        inn[:, cols] = values[0:span]
+        wide = values.astype(F32)
         for way, grow, st in ((0, widen_f, st_f), (1, widen_b, st_b)):
             scaled = (bdot(tails[...], grow[:, cols]) * wide).astype(BF16)
-            for d in range(1, GROUP):
-                st[d, :, cols] = bdot(in_turn[way, d - 1], scaled[(d - 1) * span : d * span])
+            for d in range(GROUP):
+                st[d, :, cols] = bdot(in_turn[way, d], scaled[d * span : (d + 1) * span])
 
     at = [partner(jnp.int32(d)) for d in range(GROUP)]
     none = jnp.zeros_like(last_own)
@@ -400,6 +391,8 @@
 
         return carry
 
+    for t in range(tiles):
+        w_copy(jnp.int32(t)).wait()
     project(chunk_at(zero))
     lax.fori_loop(0, chunks + STRIDE * (laps - 1), slot, 0)
 
@@ -457,8 +450,8 @@
             pltpu.VMEM((2 * heads, span), F32),
             pltpu.VMEM((2 * heads, span), F32),
             pltpu.VMEM((2 * heads, span), F32),
-            pltpu.VMEM(((GROUP - 1) * span, 4 * heads), BF16),
-            pltpu.VMEM((2, GROUP - 1, states, span), BF16),
+            pltpu.VMEM((GROUP * span, 4 * heads), BF16),
+            pltpu.VMEM((2, GROUP, states, span), BF16),
             pltpu.VMEM((chunks, states, chunk), BF16),
             pltpu.VMEM((chunks, states, chunk), BF16),
             pltpu.VMEM((chunks, states, chunk), BF16),

time: 47.1 us -> 48.1 us (1.021)
  Pallas kernels: 45 us -> 46 us
    pallas_call x1, Pallas kernels: 45 us -> 46 us  [shards(): pl.pallas_call(functools.partial(kernel, ns, nh, rows, dim, width, heads,...]
where the time goes in v9:
time: 48.1 us; the launch traced here: 47.9 us
  Pallas kernels  46 us (96%)
  local copies, waits for them, and re-layouts  1.88 us (4%)
    pallas_call x1, Pallas kernels, shards(): pl.pallas_call(functools.partial(kernel, ns, nh, rows, dim, width, heads,...  46 us
    unnamed x1, local copies, waits for them, and re-layouts  1.88 us

profile of v9, /device:TPU:0, one launch (start us, length us, event | category | flops | bytes accessed | tf_op | source)
XLA Modules:
  0.0 47.9 jit_solution(7296042793370044009)
XLA Ops:
  0.0 46.0 %shard_map.73 = bf16[128,2048]{1,0:T(8,128)(2,1)} custom-call(bf16[64,2048]{1,0:T(8,128)(2,1)} %x_ref.1, bf16[2048,2048]{1,0:T(8,128)(2,1)} %w_hbm.1, bf16[2048,512]{1,0:T(8,128)(2,1)} %wio_hbm.1, bf16[64,2048]{1,0:T(8,128)(2,1)} %bitcast.5, f32[2,32]{1,0:T(2,128)} %bias_ref.1, f32[1,32]{1,0:T(1,128)} %bitcast.6, f32[1,32]{1,0:T(1,128)} %bitcast.7), custom_call_target="tpu_custom_call" | custom-call | tf_op jit(solution)/shard_map/pallas_call | solution.py:433
  46.0 1.9 %copy.9 = bf16[128,2048]{1,0:T(8,128)(2,1)} copy(bf16[128,2048]{1,0:T(8,128)(2,1)} %shard_map.73) | data formatting | bytes 1048576

commit v10 on v8

--- a/solution.py
+++ b/solution.py
@@ -10,6 +10,7 @@
 HEADDIM = 64
 GROUP = 4
 STRIDE = 2
+LATER = 3
 MESH = pl.DeviceIdType.MESH
 F32 = jnp.float32
 BF16 = jnp.bfloat16
@@ -358,9 +359,10 @@
 
     lag_f = STRIDE * lap
     lag_b = STRIDE * (laps - 1 - lap)
-    lag = jnp.maximum(lag_f, lag_b)
     not_first = lap > 0
     not_last = lap < laps - 1
+    later = jnp.where(not_first & not_last, LATER, 0)
+    lag = jnp.maximum(lag_f, lag_b) + later
 
     def slot(n, carry):
         pass_on(
@@ -401,7 +403,7 @@
         return carry
 
     project(chunk_at(zero))
-    lax.fori_loop(0, chunks + STRIDE * (laps - 1), slot, 0)
+    lax.fori_loop(0, chunks + STRIDE * (laps - 1) + LATER, slot, 0)
 
     for d in range(1, GROUP):
         peer(jnp.int32(d)).wait_send()

time: 47.1 us -> 45.7 us (0.970)
  Pallas kernels: 45 us -> 43.6 us
    pallas_call x1, Pallas kernels: 45 us -> 43.6 us  [shards(): pl.pallas_call(functools.partial(kernel, ns, nh, rows, dim, width, heads,...]
where the time goes in v10:
time: 45.7 us; the launch traced here: 45.5 us
  Pallas kernels  43.6 us (95%)
  local copies, waits for them, and re-layouts  1.88 us (4%)
    pallas_call x1, Pallas kernels, shards(): pl.pallas_call(functools.partial(kernel, ns, nh, rows, dim, width, heads,...  43.6 us
    unnamed x1, local copies, waits for them, and re-layouts  1.88 us

profile of v10, /device:TPU:0, one launch (start us, length us, event | category | flops | bytes accessed | tf_op | source)
XLA Modules:
  0.0 45.5 jit_solution(2146960172855929564)
XLA Ops:
  0.0 43.6 %shard_map.73 = bf16[128,2048]{1,0:T(8,128)(2,1)} custom-call(bf16[64,2048]{1,0:T(8,128)(2,1)} %x_ref.1, bf16[2048,2048]{1,0:T(8,128)(2,1)} %w_hbm.1, bf16[2048,512]{1,0:T(8,128)(2,1)} %wio_hbm.1, bf16[64,2048]{1,0:T(8,128)(2,1)} %bitcast.5, f32[2,32]{1,0:T(2,128)} %bias_ref.1, f32[1,32]{1,0:T(1,128)} %bitcast.6, f32[1,32]{1,0:T(1,128)} %bitcast.7), custom_call_target="tpu_custom_call" | custom-call | tf_op jit(solution)/shard_map/pallas_call | solution.py:442
  43.6 1.9 %copy.9 = bf16[128,2048]{1,0:T(8,128)(2,1)} copy(bf16[128,2048]{1,0:T(8,128)(2,1)} %shard_map.73) | data formatting | bytes 1048576
